TPU v7x, 256 devices: a whole 4x4x8 slice. The times are simulated.
256 devices in a mesh: shift: 2 (over core), row: 32 (over z, x), col: 4 (over y).
Axes of the slice: x: 4, y: 4, z: 8, core: 2. Of those that a mesh axis runs over, the one named last changes fastest.
Arguments:
- root_inverse: float32 [8192, 4096], P(('shift', 'row'), 'col'), parts along dimension 0, may hold values from -12 to 12, as said below
- pattern: int32 [16], P('shift'), parts along dimension 0, may hold values from 0 to 15
- child_rows: float32 [2048, 4096], P(('shift', 'row'), 'col'), parts along dimension 0, may hold values from -1.5 to 1.5
- child_inverse: float32 [8192, 4096], P(('shift', 'row'), 'col'), parts along dimension 0, may hold values from -12 to 12
Outputs:
- coupling: float32 [2048, 4096], P(('shift', 'row'), 'col'), parts along dimension 0
- selected_inverse: float32 [8192, 4096], P(('shift', 'row'), 'col'), parts along dimension 0
There are 2 independent parts, one for each index of `shift`. A program takes and returns all parts, laid end to end along the dimension named above; each array names one. Nothing has to cross between parts.
Inputs may be any that keep to these rules, and one draw needn't show every extreme that they name: `root_inverse`: a symmetric matrix.
All inputs are finite; a program needn't handle non-finite values.
Results may differ from a plain program's by a relative error of at most 0.00011.
Values sent between devices are 32-bit elements; how exact they have to be, the bound alone decides.
No kernel may reach another device: no remote copies, remote signals or barrier semaphores. Data moves between devices by JAX's collectives and lax.ppermute only.
A program may use at most 64 MiB of HBM per device.

v0:
```python
import jax
import jax.numpy as jnp
from jax import lax
from jax.sharding import PartitionSpec as P

B = 128


def shards(root_inverse, pattern, child_rows, child_inverse):
    rows_dev = child_rows.shape[0]
    row_position = lax.axis_index("row")
    within = jnp.arange(B, dtype=jnp.int32)
    root_index = (pattern[:, None] * B + within[None, :]).reshape(-1)
    wanted = lax.dynamic_slice_in_dim(root_index, row_position * rows_dev, rows_dev)
    shard_cols = root_inverse.shape[1]
    portion = lax.all_gather(root_inverse, "row", axis=0, tiled=True)
    offset = wanted
    inside = (offset >= 0) & (offset < portion.shape[0])
    fetched = jnp.take(portion, jnp.clip(offset, 0, portion.shape[0] - 1), axis=0)
    selected_rows = jnp.where(
        inside[:, None], fetched, jnp.zeros((rows_dev, shard_cols), jnp.float32)
    )
    portion = lax.all_gather(selected_rows, "col", axis=1, tiled=True)
    offset = root_index
    inside = (offset >= 0) & (offset < portion.shape[1])
    fetched = jnp.take(portion, jnp.clip(offset, 0, portion.shape[1] - 1), axis=1)
    picked = jnp.where(
        inside[None, :], fetched, jnp.zeros((rows_dev, root_index.shape[0]), jnp.float32)
    )
    factor_cols = picked
    coupling = jnp.zeros((rows_dev, child_rows.shape[1]), jnp.float32) - jnp.dot(
        factor_cols,
        lax.all_gather(child_rows, "row", axis=0, tiled=True),
        precision=lax.Precision.HIGHEST,
        preferred_element_type=jnp.float32,
    )
    widened = lax.all_gather(coupling, "col", axis=1, tiled=True)
    factor_cols = widened
    correction = lax.psum_scatter(
        lax.dot_general(
            factor_cols,
            child_rows,
            (((0,), (0,)), ((), ())),
            precision=lax.Precision.HIGHEST,
            preferred_element_type=jnp.float32,
        ),
        "row",
        scatter_dimension=0,
        tiled=True,
    )
    return (coupling, child_inverse - correction)


def solution(mesh):
    return jax.shard_map(
        shards,
        mesh=mesh,
        in_specs=(
            P(("shift", "row"), "col"),
            P("shift"),
            P(("shift", "row"), "col"),
            P(("shift", "row"), "col"),
        ),
        out_specs=(P(("shift", "row"), "col"), P(("shift", "row"), "col")),
        check_vma=False,
    )
```

profile of v0, /device:TPU:8, one launch (start us, length us, event | category | flops | bytes accessed | tf_op | source)
XLA Modules:
  0.0 520.4 jit_solution(15687542516313754410)
XLA Ops:
  7.2 0.0 all-gather.3.cloned.1.call-start
  7.2 0.7 all-gather.3.cloned.1.call-update
  7.9 0.0 all-gather.5.cloned.1.call-start
  7.9 0.7 all-gather.5.cloned.1.call-update
  8.6 0.0 reduce-scatter.2.cloned.1.call-start
  8.7 0.7 broadcast_multiply_fusion
  9.4 0.1 fusion.6
  9.4 0.1 compare_and_fusion
  9.5 0.1 fusion.12
  9.6 144.4 %all-gather.3.cloned.1.call-done = f32[4096,1024]{1,0:T(8,128)} async-done(((f32[128,1024]{1,0:T(8,128)}), f32[4096,1024]{1,0:T(8,128)}) %all-gather.3.cloned.1.call-update) | async-done | bytes 16777232 | tf_op jit(solution)/shard_map/all_gather | solution.py:16
  154.0 6.4 %gather_fusion = f32[32,1024]{1,0:T(8,128)S(1)} fusion(f32[4096,1024]{1,0:T(8,128)} %all-gather.3.cloned.1.call-done, s32[1024]{0:T(1024)S(1)} %pad_clamp_fusion), kind=kCustom, calls=%fused_computation | custom fusion | bytes 262272 | tf_op jit(solution)/shard_map/jit(_take)/gather | solution.py:19
  160.5 0.1 select_select_fusion
  160.6 13.4 %all_gather.13 = f32[32,4096]{1,0:T(8,128)S(1)} all-gather(f32[32,1024]{1,0:T(8,128)S(1)} %select_select_fusion), channel_id=1, replica_groups=mesh['shift'=2,'row'=32,'col'=4] {'col'}, dimensions={1}, use_global_device_ids=true | all-gather | bytes 655360 | tf_op jit(solution)/shard_map/all_gather | solution.py:23
  173.9 0.0 copy-start
  173.9 0.6 copy.6
  174.5 2.8 gather_fusion.1
  177.3 58.2 %all-gather.5.cloned.1.call-done = f32[1024,1024]{1,0:T(8,128)} async-done(((f32[32,1024]{1,0:T(8,128)}), f32[1024,1024]{1,0:T(8,128)}) %all-gather.5.cloned.1.call-update) | async-done | bytes 4194320 | tf_op jit(solution)/shard_map/all_gather | solution.py:33
  235.5 4.9 convolution_subtract_fusion
  240.4 0.0 copy-start.2
  240.4 12.8 %all_gather.15 = f32[32,4096]{1,0:T(8,128)S(1)} all-gather(f32[32,1024]{1,0:T(8,128)S(1)} %convolution_subtract_fusion), channel_id=1, replica_groups=mesh['shift'=2,'row'=32,'col'=4] {'col'}, dimensions={1}, use_global_device_ids=true | all-gather | bytes 655360 | tf_op jit(solution)/shard_map/all_gather | solution.py:37
  253.3 0.0 copy-done
  253.3 15.8 %fusion.16 = f32[4096,1024]{1,0:T(8,128)} fusion(f32[32,4096]{1,0:T(8,128)S(1)} %all_gather.15, f32[32,1024]{1,0:T(8,128)S(1)} %copy-done), kind=kOutput, calls=%fused_computation.29 | convolution fusion | flops 1610612736 | bytes 17432576 | tf_op jit(solution)/shard_map/dot_general | solution.py:40
  269.1 0.0 copy-done.2
  269.1 0.0 copy-start.1
  269.1 0.0 reduce-scatter.2.cloned.1.call-update
  269.1 242.9 %reduce-scatter.2.cloned.1.call-done = f32[128,1024]{1,0:T(8,128)} async-done(((f32[4096,1024]{1,0:T(8,128)}), f32[128,1024]{1,0:T(8,128)}) %reduce-scatter.2.cloned.1.call-update) | async-done | bytes 524304 | tf_op jit(solution)/shard_map/reduce_scatter | solution.py:39
  512.0 0.0 copy-done.1
  512.0 1.9 sub.7
  (3 shorter events, 0.0 us)
Async XLA Ops:
  7.2 146.9 %all-gather.3.cloned.1.call-start = ((), (), s32[]{:S(2)}) async-start(), calls=%async_computation.1 | async-start | bytes 17301504 | tf_op jit(solution)/shard_map/all_gather | solution.py:16
  7.9 227.6 %all-gather.5.cloned.1.call-start = ((), (), s32[]{:S(2)}) async-start(), calls=%async_computation.2 | async-start | bytes 4325376 | tf_op jit(solution)/shard_map/all_gather | solution.py:33
  8.6 503.4 %reduce-scatter.2.cloned.1.call-start = ((), (), s32[]{:S(2)}) async-start(), calls=%async_computation.3 | async-start | bytes 17301504 | tf_op jit(solution)/shard_map/reduce_scatter | solution.py:39
  173.9 79.3 %copy-start = (f32[32,1024]{1,0:T(8,128)S(1)}, f32[32,1024]{1,0:T(8,128)}, u32[]{:S(2)}) copy-start(f32[32,1024]{1,0:T(8,128)} %param.6) | copy-start | bytes 393220
  240.4 28.7 %copy-start.2 = (f32[32,1024]{1,0:T(8,128)}, f32[32,1024]{1,0:T(8,128)S(1)}, u32[]{:S(2)}) copy-start(f32[32,1024]{1,0:T(8,128)S(1)} %convolution_subtract_fusion) | copy-start | bytes 393220
  269.1 242.9 %copy-start.1 = (f32[128,1024]{1,0:T(8,128)S(1)}, f32[128,1024]{1,0:T(8,128)}, u32[]{:S(2)}) copy-start(f32[128,1024]{1,0:T(8,128)} %param.7) | copy-start | bytes 1572868
Sparse Core Ops, SparseCore 0:
  10.6 143.4 all-gather.2
  156.6 78.8 all-gather.4
  269.3 242.7 reduce-scatter.1
where the time goes:
time: 521 us; the launch traced here: 520 us
  waiting for transfers between devices  447 us (86%)
  blocking collectives  26.2 us (5%)
  matrix products  20.7 us (4%)
  between operations  13.8 us (3%)
  local copies, waits for them, and re-layouts  9.86 us (2%)
    reduce_scatter x1, waiting for transfers between devices, shards(): lax.psum_scatter(lax.dot_general(factor_cols, child_rows, (((0,), (0,)),...  243 us
    all_gather x1, waiting for transfers between devices, shards(): portion = lax.all_gather(root_inverse, 'row', axis=0, tiled=True)  144 us
    all_gather x1, waiting for transfers between devices, shards(): lax.all_gather(child_rows, 'row', axis=0, tiled=True)  58.2 us
    dot_general x1, matrix products, shards(): lax.dot_general(factor_cols, child_rows, (((0,), (0,)), ((), ())), precis...  15.8 us
    all_gather x1, blocking collectives, shards(): portion = lax.all_gather(selected_rows, 'col', axis=1, tiled=True)  13.4 us
    all_gather x1, blocking collectives, shards(): widened = lax.all_gather(coupling, 'col', axis=1, tiled=True)  12.8 us
  transfers between devices with their start and end apart: 3, of which 3 were waited for; matrix products, arithmetic and copies ran while one was open for 2% of the time, Pallas kernels for 0%

commit v1 on v0

v1 whole, which is shorter than its diff:
```python
import jax
import jax.numpy as jnp
from jax import lax
from jax.sharding import Mesh, PartitionSpec as P

B = 128
NZ, NX, NY = 8, 4, 4
HIGH = lax.Precision.HIGH


def shift_perm(n, d):
    return [(i, (i + d) % n) for i in range(n)]


def zxy(z, x, y):
    return (z * NX + x) * NY + y


def shards(root_inverse, pattern, child_rows, child_inverse):
    z = lax.axis_index("z")
    x = lax.axis_index("x")
    y = lax.axis_index("col")
    f32 = jnp.float32

    parts = [child_rows] + [
        lax.ppermute(child_rows, "x", shift_perm(NX, d)) for d in (1, 2, 3)
    ]
    block = jnp.zeros((NX, 32, 1024), f32)
    for d in range(NX):
        block = lax.dynamic_update_slice(
            block, parts[d][None], (lax.rem(x + NX - d, NX), 0, 0)
        )
    gathered = lax.all_gather(block.reshape(128, 1024), "z", axis=0, tiled=True)

    e = lax.rem(z, 2)
    perm = [
        (zxy(a, b, c), zxy(2 * c + a // 4, b, a % 4))
        for a in range(NZ) for b in range(NX) for c in range(NY)
    ]
    turned = lax.ppermute(child_rows, ("z", "x", "col"), perm).reshape(32, 2, 512)
    mine = lax.dynamic_slice_in_dim(turned, e, 1, axis=1).reshape(32, 512)
    other = lax.dynamic_slice_in_dim(turned, 1 - e, 1, axis=1).reshape(32, 512)
    other = lax.ppermute(other, "z", [(i, i ^ 1) for i in range(NZ)])
    pair = jnp.where(e == 0, jnp.stack([mine, other]), jnp.stack([other, mine]))
    strip = jnp.zeros((2, 4, 32, 512), f32)
    for d in range(NY):
        got = pair if d == 0 else lax.ppermute(pair, "col", shift_perm(NY, d))
        strip = lax.dynamic_update_slice(
            strip, got[:, None], (0, lax.rem(y + NY - d, NY), 0, 0)
        )
    strip = strip.reshape(256, 512)

    blocks = root_inverse.reshape(B, 8, B)

    def listed(target):
        out = []
        for h in range(2):
            k = lax.dynamic_index_in_dim(pattern, 2 * target + h, 0, False) - 8 * y
            ok = (k >= 0) & (k < 8)
            col = lax.dynamic_slice_in_dim(blocks, jnp.clip(k, 0, 7), 1, axis=1)
            out.append(jnp.where(ok, col.reshape(B, B), 0.0))
        return jnp.stack(out)

    cols = listed(y)
    for d in (1, 2, 3):
        sent = listed(lax.rem(y + d, NY))
        pairs = [
            (a * NY + c, a * NY + (c + d) % NY) for a in range(4) for c in range(2)
        ]
        cols = cols + lax.ppermute(sent, ("z", "col"), pairs)

    cut = cols.reshape(2, NX, 4, 8, B).transpose(0, 2, 1, 3, 4).reshape(32 * 8, B)
    cut = lax.all_to_all(cut, ("z", "x"), 0, 0, tiled=True).reshape(32, 8, B)
    kept = jnp.concatenate(
        [lax.dynamic_slice_in_dim(cut, pattern[j], 1, axis=0) for j in range(8)]
    )
    wide = jnp.broadcast_to(kept[None], (NZ, 8, 8, B)).reshape(NZ * 64, B)
    wide = lax.all_to_all(wide, "z", 0, 0, tiled=True)
    picked = (
        wide.reshape(2, 4, 8, 8, B).transpose(2, 1, 3, 0, 4).reshape(256, 256)
    )
    rows = lax.dynamic_slice_in_dim(picked, z * 32, 32, axis=0)

    share = lax.dot_general(
        picked, strip, (((0,), (0,)), ((), ())), precision=HIGH,
        preferred_element_type=f32,
    ).reshape(256, NX, B)

    def share_of(t):
        return lax.dynamic_slice_in_dim(share, t, 1, axis=1).reshape(256, B)

    total = share_of(x)
    for d in (1, 2, 3):
        total = total + lax.ppermute(
            share_of(lax.rem(x + d, NX)), "x", shift_perm(NX, d)
        )

    both = jnp.concatenate([total, rows.reshape(32, 2, B).transpose(1, 0, 2).reshape(64, B)])
    full = jnp.zeros((NY, 320, B), f32)
    for d in range(NY):
        got = both if d == 0 else lax.ppermute(both, "col", shift_perm(NY, d))
        full = lax.dynamic_update_slice(full, got[None], (lax.rem(y + NY - d, NY), 0, 0))
    product = full[:, :256].reshape(1024, B)
    picked_rows = full[:, 256:].reshape(NY * 2, 32, B).transpose(1, 0, 2).reshape(32, 1024)

    coupling = -jnp.dot(
        picked_rows, gathered, precision=HIGH, preferred_element_type=f32
    )
    correction = lax.dot_general(
        product, gathered, (((0,), (0,)), ((), ())), precision=HIGH,
        preferred_element_type=f32,
    )
    return coupling, child_inverse + correction


def solution(mesh):
    inner = Mesh(mesh.devices.reshape(2, NZ, NX, NY), ("shift", "z", "x", "col"))
    whole = P(("shift", "z", "x"), "col")
    return jax.shard_map(
        shards,
        mesh=inner,
        in_specs=(whole, P("shift"), whole, whole),
        out_specs=(whole, whole),
        check_vma=False,
    )
```

time: 521 us -> 129 us (0.25)
  waiting for transfers between devices: 447 us -> 32.6 us
  starting transfers between devices: 0.11 us -> 45.9 us
  blocking collectives: 26.2 us -> 0 us
  between operations: 13.8 us -> 34.5 us
  matrix products: 20.7 us -> 7.26 us
    reduce_scatter x1 -> x0, waiting for transfers between devices: 243 us -> none  [shards(): lax.psum_scatter(lax.dot_general(factor_cols, child_rows, (((0,), (0,)),...]
    all_gather x2 -> x1, waiting for transfers between devices: 203 us -> 0.02 us  [shards(): gathered = lax.all_gather(block.reshape(128, 1024), 'z', axis=0, tiled=True)]
    ppermute x0 -> x17, starting transfers between devices: none -> 37.2 us  [the longest x3 11.7 us: shards(): cols = cols + lax.ppermute(sent, ('z', 'col'), pairs)]
    all_gather x2 -> x0, blocking collectives: 26.2 us -> none  [the longest x1 13.4 us: shards(): portion = lax.all_gather(selected_rows, 'col', axis=1, tiled=True)]
    all_to_all x0 -> x2, waiting for transfers between devices: none -> 17.2 us  [the longest x1 10.1 us: shards(): wide = lax.all_to_all(wide, 'z', 0, 0, tiled=True)]
    ppermute x0 -> x17, waiting for transfers between devices: none -> 15.4 us  [the longest x3 6.1 us: shards(): got = both if d == 0 else lax.ppermute(both, 'col', shift_perm(NY, d))]
    dot_general x2 -> x3, matrix products: 20.7 us -> 7.26 us  [the longest x1 4.32 us: shards(): jnp.dot(picked_rows, gathered, precision=HIGH, preferred_element_type=f32)]
    gather x2 -> x0, local copies, waits for them, and re-layouts: 9.24 us -> none  [the longest x1 6.44 us: shards(): jnp.take(portion, jnp.clip(offset, 0, portion.shape[0] - 1), axis=0)]
  transfers between devices with their start and end apart: 3 -> 20, of which waited for: 3 -> 9; matrix products, arithmetic and copies ran while one was open for 2% -> 6% of each run, Pallas kernels for 0% -> 0%
where the time goes in v1:
time: 129 us; the launch traced here: 128 us
  starting transfers between devices  45.9 us (36%)
  between operations  34.5 us (27%)
  waiting for transfers between devices  32.6 us (25%)
  local copies, waits for them, and re-layouts  7.32 us (6%)
  matrix products  7.26 us (6%)
    ppermute x3, starting transfers between devices, shards(): cols = cols + lax.ppermute(sent, ('z', 'col'), pairs)  11.7 us
    all_to_all x1, waiting for transfers between devices, shards(): wide = lax.all_to_all(wide, 'z', 0, 0, tiled=True)  10.1 us
    all_to_all x1, waiting for transfers between devices, shards(): cut = lax.all_to_all(cut, ('z', 'x'), 0, 0, tiled=True).reshape(32, 8, B)  7.09 us
    ppermute x3, waiting for transfers between devices, shards(): got = both if d == 0 else lax.ppermute(both, 'col', shift_perm(NY, d))  6.1 us
    ppermute x3, starting transfers between devices, shards(): lax.ppermute(child_rows, 'x', shift_perm(NX, d))  5.73 us
    ppermute x3, waiting for transfers between devices, shards(): lax.ppermute(share_of(lax.rem(x + d, NX)), 'x', shift_perm(NX, d))  5.47 us
    all_to_all x1, starting transfers between devices, shards(): cut = lax.all_to_all(cut, ('z', 'x'), 0, 0, tiled=True).reshape(32, 8, B)  5.3 us
    ppermute x1, starting transfers between devices, shards(): lax.ppermute(child_rows, ('z', 'x', 'col'), perm).reshape(32, 2, 512)  5.07 us
  transfers between devices with their start and end apart: 20, of which 9 were waited for; matrix products, arithmetic and copies ran while one was open for 6% of the time, Pallas kernels for 0%

profile of v1, /device:TPU:8, one launch (start us, length us, event | category | flops | bytes accessed | tf_op | source)
XLA Modules:
  0.0 127.8 jit_solution(223280629660531931)
XLA Ops:
  7.2 1.6 %collective-permute-start.14 = (f32[32,1024]{1,0:T(8,128)}, f32[32,1024]{1,0:T(8,128)S(1)}, u32[]{:S(2)}, u32[]{:S(2)}) collective-permute-start(f32[32,1024]{1,0:T(8,128)} %param.6), channel_id=1, source_target_pairs={{0,4},{4,8},{8,12},{12,0},{1,5},{5,9},{9,13},{13,1},{2,6},{6,10},{... | collective-permute-start | bytes 393224 | tf_op jit(solution)/shard_map/ppermute | solution.py:26
  8.8 2.7 %collective-permute-start.15 = (f32[32,1024]{1,0:T(8,128)}, f32[32,1024]{1,0:T(8,128)S(1)}, u32[]{:S(2)}, u32[]{:S(2)}) collective-permute-start(f32[32,1024]{1,0:T(8,128)} %param.6), channel_id=1, source_target_pairs={{0,8},{4,12},{8,0},{12,4},{1,9},{5,13},{9,1},{13,5},{2,10},{6,14},... | collective-permute-start | bytes 393224 | tf_op jit(solution)/shard_map/ppermute | solution.py:26
  11.5 1.4 %collective-permute-start.16 = (f32[32,1024]{1,0:T(8,128)}, f32[32,1024]{1,0:T(8,128)S(1)}, u32[]{:S(2)}, u32[]{:S(2)}) collective-permute-start(f32[32,1024]{1,0:T(8,128)} %param.6), channel_id=1, source_target_pairs={{0,12},{4,0},{8,4},{12,8},{1,13},{5,1},{9,5},{13,9},{2,14},{6,2},{... | collective-permute-start | bytes 393224 | tf_op jit(solution)/shard_map/ppermute | solution.py:26
  13.0 0.9 bitcast_dynamic-update-slice_fusion.10
  14.1 3.6 %collective-permute-done.15 = f32[32,1024]{1,0:T(8,128)S(1)} collective-permute-done((f32[32,1024]{1,0:T(8,128)}, f32[32,1024]{1,0:T(8,128)S(1)}, u32[]{:S(2)}, u32[]{:S(2)}) %collective-permute-start.15) | collective-permute-done | bytes 131104 | tf_op jit(solution)/shard_map/ppermute | solution.py:26
  17.8 0.8 copy-done.1
  18.6 5.1 %collective-permute-start.3 = (f32[32,1024]{1,0:T(8,128)}, f32[32,1024]{1,0:T(8,128)S(1)}, u32[]{:S(2)}, u32[]{:S(2)}) collective-permute-start(f32[32,1024]{1,0:T(8,128)} %param.6), channel_id=1, source_target_pairs={{0,0},{1,32},{2,64},{3,96},{4,4},{5,36},{6,68},{7,100},{8,8},{9,40... | collective-permute-start | bytes 393224 | tf_op jit(solution)/shard_map/ppermute | solution.py:40
  23.7 2.0 %fusion.7 = (s32[1]{0:T(128)}, s32[1]{0:T(128)}, s32[1]{0:T(128)}, s32[1]{0:T(128)}, s32[1]{0:T(128)}, /*index=5*/s32[1]{0:T(128)}, s32[1]{0:T(128)}, s32[1]{0:T...) fusion(s32[8]{0:T(128)} %param.5, ...), kind=kLoop, calls=%fused_computation.61 | loop fusion | bytes 160 | tf_op jit(solution)/shard_map/slice | solution.py:75
  30.8 1.2 copy.44
  32.2 7.3 %collective-permute-start = (f32[2,128,128]{1,2,0:T(8,128)S(1)}, f32[2,128,128]{1,2,0:T(8,128)S(1)}, u32[]{:S(2)}, u32[]{:S(2)}) collective-permute-start(f32[2,128,128]{1,2,0:T(8,128)S(1)} %pad_maximum_fusion.1), channel_id=1, source_target_pairs={{0,1},{1,2},{16,17},{17,18},{32,33},{33,34},{48,49},{49,50},{4,5},... | collective-permute-start | bytes 393224 | tf_op jit(solution)/shard_map/ppermute | solution.py:70
  39.5 1.3 %collective-permute-start.1 = (f32[2,128,128]{1,2,0:T(8,128)S(1)}, f32[2,128,128]{1,2,0:T(8,128)S(1)}, u32[]{:S(2)}, u32[]{:S(2)}) collective-permute-start(f32[2,128,128]{1,2,0:T(8,128)S(1)} %pad_maximum_fusion.2), channel_id=1, source_target_pairs={{0,2},{1,3},{16,18},{17,19},{32,34},{33,35},{48,50},{49,51},{4,6},... | collective-permute-start | bytes 393224 | tf_op jit(solution)/shard_map/ppermute | solution.py:70
  41.1 1.7 %collective-permute-start.4 = (f32[32,512]{1,0:T(8,128)S(1)}, f32[32,512]{1,0:T(8,128)S(1)}, u32[]{:S(2)}, u32[]{:S(2)}) collective-permute-start(f32[32,512]{1,0:T(8,128)S(1)} %bitcast.131), channel_id=1, source_target_pairs={{0,16},{16,0},{32,48},{48,32},{64,80},{80,64},{96,112},{112,96},{1... | collective-permute-start | bytes 196616 | tf_op jit(solution)/shard_map/ppermute | solution.py:43
  42.7 3.1 %collective-permute-start.2 = (f32[2,128,128]{1,2,0:T(8,128)S(1)}, f32[2,128,128]{1,2,0:T(8,128)S(1)}, u32[]{:S(2)}, u32[]{:S(2)}) collective-permute-start(f32[2,128,128]{1,2,0:T(8,128)S(1)} %pad_maximum_fusion.3), channel_id=1, source_target_pairs={{0,3},{1,0},{16,19},{17,16},{32,35},{33,32},{48,51},{49,48},{4,7},... | collective-permute-start | bytes 393224 | tf_op jit(solution)/shard_map/ppermute | solution.py:70
  61.6 5.3 %all-to-all-start = ((f32[32,8,128]{2,1,0:T(8,128)}), f32[32,8,128]{2,1,0:T(8,128)S(1)}, u32[]{:S(2)}, u32[]{:S(2)}) async-start(f32[32,8,128]{2,1,0:T(8,128)} %bitcast.19), calls=%async_computation | async-start | bytes 262144 | tf_op jit(solution)/shard_map/all_to_all | solution.py:73
  66.9 2.1 %collective-permute-start.6 = (f32[2,32,512]{2,1,0:T(8,128)S(1)}, f32[2,32,512]{2,1,0:T(8,128)S(1)}, u32[]{:S(2)}, u32[]{:S(2)}) collective-permute-start(f32[2,32,512]{2,1,0:T(8,128)S(1)} %maximum_select_fusion.1), channel_id=1, source_target_pairs={{0,2},{1,3},{2,0},{3,1},{4,6},{5,7},{6,4},{7,5},{8,10},{9,11},{10,... | collective-permute-start | bytes 393224 | tf_op jit(solution)/shard_map/ppermute | solution.py:47
  69.1 2.5 %collective-permute-start.7 = (f32[2,32,512]{2,1,0:T(8,128)S(1)}, f32[2,32,512]{2,1,0:T(8,128)S(1)}, u32[]{:S(2)}, u32[]{:S(2)}) collective-permute-start(f32[2,32,512]{2,1,0:T(8,128)S(1)} %maximum_select_fusion.1), channel_id=1, source_target_pairs={{0,3},{1,0},{2,1},{3,2},{4,7},{5,4},{6,5},{7,6},{8,11},{9,8},{10,9... | collective-permute-start | bytes 393224 | tf_op jit(solution)/shard_map/ppermute | solution.py:47
  71.7 7.1 %all-to-all-done = f32[32,8,128]{2,1,0:T(8,128)S(1)} async-done(((f32[32,8,128]{2,1,0:T(8,128)}), f32[32,8,128]{2,1,0:T(8,128)S(1)}, u32[]{:S(2)}, u32[]{:S(2)}) %all-to-all-start) | async-done | bytes 131104 | tf_op jit(solution)/shard_map/all_to_all | solution.py:73
  78.8 0.7 broadcast_in_dim.65
  79.6 3.4 %all-to-all-start.1 = ((f32[8,64,128]{2,1,0:T(8,128)}), f32[8,64,128]{2,1,0:T(8,128)S(1)}, u32[]{:S(2)}, u32[]{:S(2)}) async-start(f32[8,64,128]{2,1,0:T(8,128)} %broadcast_in_dim.65), calls=%async_computation.1 | async-start | bytes 524288 | tf_op jit(solution)/shard_map/all_to_all | solution.py:78
  83.3 10.1 %all-to-all-done.1 = f32[8,64,128]{2,1,0:T(8,128)S(1)} async-done(((f32[8,64,128]{2,1,0:T(8,128)}), f32[8,64,128]{2,1,0:T(8,128)S(1)}, u32[]{:S(2)}, u32[]{:S(2)}) %all-to-all-start.1) | async-done | bytes 262176 | tf_op jit(solution)/shard_map/all_to_all | solution.py:78
  94.1 1.3 %collective-permute-start.10 = (f32[256,128]{1,0:T(8,128)S(1)}, f32[256,128]{1,0:T(8,128)S(1)}, u32[]{:S(2)}, u32[]{:S(2)}) collective-permute-start(f32[256,128]{1,0:T(8,128)S(1)} %get-tuple-element.3), channel_id=1, source_target_pairs={{0,12},{4,0},{8,4},{12,8},{1,13},{5,1},{9,5},{13,9},{2,14},{6,2},{... | collective-permute-start | bytes 393224 | tf_op jit(solution)/shard_map/ppermute | solution.py:94
  95.4 0.8 collective-permute-start.8
  96.2 1.3 %collective-permute-start.9 = (f32[256,128]{1,0:T(8,128)S(1)}, f32[256,128]{1,0:T(8,128)S(1)}, u32[]{:S(2)}, u32[]{:S(2)}) collective-permute-start(f32[256,128]{1,0:T(8,128)S(1)} %get-tuple-element.4), channel_id=1, source_target_pairs={{0,8},{4,12},{8,0},{12,4},{1,9},{5,13},{9,1},{13,5},{2,10},{6,14},... | collective-permute-start | bytes 393224 | tf_op jit(solution)/shard_map/ppermute | solution.py:94
  97.5 1.6 %collective-permute-done.10 = f32[256,128]{1,0:T(8,128)S(1)} collective-permute-done((f32[256,128]{1,0:T(8,128)S(1)}, f32[256,128]{1,0:T(8,128)S(1)}, u32[]{:S(2)}, u32[]{:S(2)}) %collective-permute-start.10) | collective-permute-done | bytes 131104 | tf_op jit(solution)/shard_map/ppermute | solution.py:94
  99.1 3.9 %collective-permute-done.8 = f32[256,128]{1,0:T(8,128)S(1)} collective-permute-done((f32[256,128]{1,0:T(8,128)S(1)}, f32[256,128]{1,0:T(8,128)S(1)}, u32[]{:S(2)}, u32[]{:S(2)}) %collective-permute-start.8) | collective-permute-done | bytes 131104 | tf_op jit(solution)/shard_map/ppermute | solution.py:94
  103.1 2.6 %collective-permute-start.11 = (f32[320,128]{1,0:T(8,128)S(1)}, f32[320,128]{1,0:T(8,128)S(1)}, u32[]{:S(2)}, u32[]{:S(2)}) collective-permute-start(f32[320,128]{1,0:T(8,128)S(1)} %pad_maximum_fusion), channel_id=1, source_target_pairs={{0,1},{1,2},{2,3},{3,0},{4,5},{5,6},{6,7},{7,4},{8,9},{9,10},{10,1... | collective-permute-start | bytes 491528 | tf_op jit(solution)/shard_map/ppermute | solution.py:101
  105.7 1.6 %collective-permute-start.12 = (f32[320,128]{1,0:T(8,128)S(1)}, f32[320,128]{1,0:T(8,128)S(1)}, u32[]{:S(2)}, u32[]{:S(2)}) collective-permute-start(f32[320,128]{1,0:T(8,128)S(1)} %pad_maximum_fusion), channel_id=1, source_target_pairs={{0,2},{1,3},{2,0},{3,1},{4,6},{5,7},{6,4},{7,5},{8,10},{9,11},{10,... | collective-permute-start | bytes 491528 | tf_op jit(solution)/shard_map/ppermute | solution.py:101
  107.2 0.8 collective-permute-start.13
  108.5 4.1 %collective-permute-done.12 = f32[320,128]{1,0:T(8,128)S(1)} collective-permute-done((f32[320,128]{1,0:T(8,128)S(1)}, f32[320,128]{1,0:T(8,128)S(1)}, u32[]{:S(2)}, u32[]{:S(2)}) %collective-permute-start.12) | collective-permute-done | bytes 163872 | tf_op jit(solution)/shard_map/ppermute | solution.py:101
  112.6 1.6 %collective-permute-done.13 = f32[320,128]{1,0:T(8,128)S(1)} collective-permute-done((f32[320,128]{1,0:T(8,128)S(1)}, f32[320,128]{1,0:T(8,128)S(1)}, u32[]{:S(2)}, u32[]{:S(2)}) %collective-permute-start.13) | collective-permute-done | bytes 163872 | tf_op jit(solution)/shard_map/ppermute | solution.py:101
  114.3 4.3 %convolution_negate_fusion = f32[32,1024]{1,0:T(8,128)} fusion(f32[1024,1024]{1,0:T(8,128)} %all-gather.2.cloned.1.call-done, f32[8,4,8,128]{3,2,1,0:T(8,128)S(1)} %bitcast.124), kind=kOutput, calls=%fused_computation.1 | convolution fusion | flops 201359360 | bytes 4456448 | tf_op jit(solution)/shard_map/dot_general | solution.py:106
  118.7 2.3 %convolution_add_fusion = f32[128,1024]{1,0:T(8,128)} fusion(f32[128,1024]{1,0:T(8,128)S(1)} %copy-done.2, f32[1024,128]{1,0:T(8,128)S(1)} %bitcast.118, f32[1024,1024]{1,0:T(8,128)S(1)} %copy-done), kind=kOutput, calls=%fused_computation | convolution fusion | flops 805437440 | bytes 5767168 | tf_op jit(solution)/shard_map/dot_general | solution.py:109
  (66 shorter events, 3.3 us)
Async XLA Ops:
  7.2 107.2 %all-gather.2.cloned.1.call-start = ((), (), s32[]{:S(2)}) async-start(), calls=%async_computation.2 | async-start | bytes 4718592 | tf_op jit(solution)/shard_map/all_gather | solution.py:33
  7.2 6.9 %collective-permute-start.14 = (f32[32,1024]{1,0:T(8,128)}, f32[32,1024]{1,0:T(8,128)S(1)}, u32[]{:S(2)}, u32[]{:S(2)}) collective-permute-start(f32[32,1024]{1,0:T(8,128)} %param.6), channel_id=1, source_target_pairs={{0,4},{4,8},{8,12},{12,0},{1,5},{5,9},{9,13},{13,1},{2,6},{6,10},{... | collective-permute-start | bytes 393224 | tf_op jit(solution)/shard_map/ppermute | solution.py:26
  8.8 9.0 %collective-permute-start.15 = (f32[32,1024]{1,0:T(8,128)}, f32[32,1024]{1,0:T(8,128)S(1)}, u32[]{:S(2)}, u32[]{:S(2)}) collective-permute-start(f32[32,1024]{1,0:T(8,128)} %param.6), channel_id=1, source_target_pairs={{0,8},{4,12},{8,0},{12,4},{1,9},{5,13},{9,1},{13,5},{2,10},{6,14},... | collective-permute-start | bytes 393224 | tf_op jit(solution)/shard_map/ppermute | solution.py:26
  11.5 6.2 %collective-permute-start.16 = (f32[32,1024]{1,0:T(8,128)}, f32[32,1024]{1,0:T(8,128)S(1)}, u32[]{:S(2)}, u32[]{:S(2)}) collective-permute-start(f32[32,1024]{1,0:T(8,128)} %param.6), channel_id=1, source_target_pairs={{0,12},{4,0},{8,4},{12,8},{1,13},{5,1},{9,5},{13,9},{2,14},{6,2},{... | collective-permute-start | bytes 393224 | tf_op jit(solution)/shard_map/ppermute | solution.py:26
  17.8 0.8 copy-start.1
  18.6 22.2 %collective-permute-start.3 = (f32[32,1024]{1,0:T(8,128)}, f32[32,1024]{1,0:T(8,128)S(1)}, u32[]{:S(2)}, u32[]{:S(2)}) collective-permute-start(f32[32,1024]{1,0:T(8,128)} %param.6), channel_id=1, source_target_pairs={{0,0},{1,32},{2,64},{3,96},{4,4},{5,36},{6,68},{7,100},{8,8},{9,40... | collective-permute-start | bytes 393224 | tf_op jit(solution)/shard_map/ppermute | solution.py:40
  32.2 28.6 %collective-permute-start = (f32[2,128,128]{1,2,0:T(8,128)S(1)}, f32[2,128,128]{1,2,0:T(8,128)S(1)}, u32[]{:S(2)}, u32[]{:S(2)}) collective-permute-start(f32[2,128,128]{1,2,0:T(8,128)S(1)} %pad_maximum_fusion.1), channel_id=1, source_target_pairs={{0,1},{1,2},{16,17},{17,18},{32,33},{33,34},{48,49},{49,50},{4,5},... | collective-permute-start | bytes 393224 | tf_op jit(solution)/shard_map/ppermute | solution.py:70
  39.5 21.3 %collective-permute-start.1 = (f32[2,128,128]{1,2,0:T(8,128)S(1)}, f32[2,128,128]{1,2,0:T(8,128)S(1)}, u32[]{:S(2)}, u32[]{:S(2)}) collective-permute-start(f32[2,128,128]{1,2,0:T(8,128)S(1)} %pad_maximum_fusion.2), channel_id=1, source_target_pairs={{0,2},{1,3},{16,18},{17,19},{32,34},{33,35},{48,50},{49,51},{4,6},... | collective-permute-start | bytes 393224 | tf_op jit(solution)/shard_map/ppermute | solution.py:70
  41.1 19.6 %collective-permute-start.4 = (f32[32,512]{1,0:T(8,128)S(1)}, f32[32,512]{1,0:T(8,128)S(1)}, u32[]{:S(2)}, u32[]{:S(2)}) collective-permute-start(f32[32,512]{1,0:T(8,128)S(1)} %bitcast.131), channel_id=1, source_target_pairs={{0,16},{16,0},{32,48},{48,32},{64,80},{80,64},{96,112},{112,96},{1... | collective-permute-start | bytes 196616 | tf_op jit(solution)/shard_map/ppermute | solution.py:43
  42.7 18.1 %collective-permute-start.2 = (f32[2,128,128]{1,2,0:T(8,128)S(1)}, f32[2,128,128]{1,2,0:T(8,128)S(1)}, u32[]{:S(2)}, u32[]{:S(2)}) collective-permute-start(f32[2,128,128]{1,2,0:T(8,128)S(1)} %pad_maximum_fusion.3), channel_id=1, source_target_pairs={{0,3},{1,0},{16,19},{17,16},{32,35},{33,32},{48,51},{49,48},{4,7},... | collective-permute-start | bytes 393224 | tf_op jit(solution)/shard_map/ppermute | solution.py:70
  60.7 10.9 %collective-permute-start.5 = (f32[2,32,512]{2,1,0:T(8,128)S(1)}, f32[2,32,512]{2,1,0:T(8,128)S(1)}, u32[]{:S(2)}, u32[]{:S(2)}) collective-permute-start(f32[2,32,512]{2,1,0:T(8,128)S(1)} %maximum_select_fusion.1), channel_id=1, source_target_pairs={{0,1},{1,2},{2,3},{3,0},{4,5},{5,6},{6,7},{7,4},{8,9},{9,10},{10,1... | collective-permute-start | bytes 393224 | tf_op jit(solution)/shard_map/ppermute | solution.py:47
  61.6 17.1 %all-to-all-start = ((f32[32,8,128]{2,1,0:T(8,128)}), f32[32,8,128]{2,1,0:T(8,128)S(1)}, u32[]{:S(2)}, u32[]{:S(2)}) async-start(f32[32,8,128]{2,1,0:T(8,128)} %bitcast.19), calls=%async_computation | async-start | bytes 262144 | tf_op jit(solution)/shard_map/all_to_all | solution.py:73
  66.9 16.1 %collective-permute-start.6 = (f32[2,32,512]{2,1,0:T(8,128)S(1)}, f32[2,32,512]{2,1,0:T(8,128)S(1)}, u32[]{:S(2)}, u32[]{:S(2)}) collective-permute-start(f32[2,32,512]{2,1,0:T(8,128)S(1)} %maximum_select_fusion.1), channel_id=1, source_target_pairs={{0,2},{1,3},{2,0},{3,1},{4,6},{5,7},{6,4},{7,5},{8,10},{9,11},{10,... | collective-permute-start | bytes 393224 | tf_op jit(solution)/shard_map/ppermute | solution.py:47
  69.1 14.0 %collective-permute-start.7 = (f32[2,32,512]{2,1,0:T(8,128)S(1)}, f32[2,32,512]{2,1,0:T(8,128)S(1)}, u32[]{:S(2)}, u32[]{:S(2)}) collective-permute-start(f32[2,32,512]{2,1,0:T(8,128)S(1)} %maximum_select_fusion.1), channel_id=1, source_target_pairs={{0,3},{1,0},{2,1},{3,2},{4,7},{5,4},{6,5},{7,6},{8,11},{9,8},{10,9... | collective-permute-start | bytes 393224 | tf_op jit(solution)/shard_map/ppermute | solution.py:47
  79.6 13.8 %all-to-all-start.1 = ((f32[8,64,128]{2,1,0:T(8,128)}), f32[8,64,128]{2,1,0:T(8,128)S(1)}, u32[]{:S(2)}, u32[]{:S(2)}) async-start(f32[8,64,128]{2,1,0:T(8,128)} %broadcast_in_dim.65), calls=%async_computation.1 | async-start | bytes 524288 | tf_op jit(solution)/shard_map/all_to_all | solution.py:78
  94.1 5.0 %collective-permute-start.10 = (f32[256,128]{1,0:T(8,128)S(1)}, f32[256,128]{1,0:T(8,128)S(1)}, u32[]{:S(2)}, u32[]{:S(2)}) collective-permute-start(f32[256,128]{1,0:T(8,128)S(1)} %get-tuple-element.3), channel_id=1, source_target_pairs={{0,12},{4,0},{8,4},{12,8},{1,13},{5,1},{9,5},{13,9},{2,14},{6,2},{... | collective-permute-start | bytes 393224 | tf_op jit(solution)/shard_map/ppermute | solution.py:94
  95.4 7.6 %collective-permute-start.8 = (f32[256,128]{1,0:T(8,128)S(1)}, f32[256,128]{1,0:T(8,128)S(1)}, u32[]{:S(2)}, u32[]{:S(2)}) collective-permute-start(f32[256,128]{1,0:T(8,128)S(1)} %get-tuple-element.2), channel_id=1, source_target_pairs={{0,4},{4,8},{8,12},{12,0},{1,5},{5,9},{9,13},{13,1},{2,6},{6,10},{... | collective-permute-start | bytes 393224 | tf_op jit(solution)/shard_map/ppermute | solution.py:94
  96.2 6.8 %collective-permute-start.9 = (f32[256,128]{1,0:T(8,128)S(1)}, f32[256,128]{1,0:T(8,128)S(1)}, u32[]{:S(2)}, u32[]{:S(2)}) collective-permute-start(f32[256,128]{1,0:T(8,128)S(1)} %get-tuple-element.4), channel_id=1, source_target_pairs={{0,8},{4,12},{8,0},{12,4},{1,9},{5,13},{9,1},{13,5},{2,10},{6,14},... | collective-permute-start | bytes 393224 | tf_op jit(solution)/shard_map/ppermute | solution.py:94
  103.0 15.6 %copy-start.2 = (f32[128,1024]{1,0:T(8,128)S(1)}, f32[128,1024]{1,0:T(8,128)}, u32[]{:S(2)}) copy-start(f32[128,1024]{1,0:T(8,128)} %param.7) | copy-start | bytes 1572868
  103.1 5.4 %collective-permute-start.11 = (f32[320,128]{1,0:T(8,128)S(1)}, f32[320,128]{1,0:T(8,128)S(1)}, u32[]{:S(2)}, u32[]{:S(2)}) collective-permute-start(f32[320,128]{1,0:T(8,128)S(1)} %pad_maximum_fusion), channel_id=1, source_target_pairs={{0,1},{1,2},{2,3},{3,0},{4,5},{5,6},{6,7},{7,4},{8,9},{9,10},{10,1... | collective-permute-start | bytes 491528 | tf_op jit(solution)/shard_map/ppermute | solution.py:101
  105.7 6.9 %collective-permute-start.12 = (f32[320,128]{1,0:T(8,128)S(1)}, f32[320,128]{1,0:T(8,128)S(1)}, u32[]{:S(2)}, u32[]{:S(2)}) collective-permute-start(f32[320,128]{1,0:T(8,128)S(1)} %pad_maximum_fusion), channel_id=1, source_target_pairs={{0,2},{1,3},{2,0},{3,1},{4,6},{5,7},{6,4},{7,5},{8,10},{9,11},{10,... | collective-permute-start | bytes 491528 | tf_op jit(solution)/shard_map/ppermute | solution.py:101
  107.2 7.0 %collective-permute-start.13 = (f32[320,128]{1,0:T(8,128)S(1)}, f32[320,128]{1,0:T(8,128)S(1)}, u32[]{:S(2)}, u32[]{:S(2)}) collective-permute-start(f32[320,128]{1,0:T(8,128)S(1)} %pad_maximum_fusion), channel_id=1, source_target_pairs={{0,3},{1,0},{2,1},{3,2},{4,7},{5,4},{6,5},{7,6},{8,11},{9,8},{10,9... | collective-permute-start | bytes 491528 | tf_op jit(solution)/shard_map/ppermute | solution.py:101
  114.3 4.3 %copy-start = (f32[1024,1024]{1,0:T(8,128)S(1)}, f32[1024,1024]{1,0:T(8,128)}, u32[]{:S(2)}) copy-start(f32[1024,1024]{1,0:T(8,128)} %all-gather.2.cloned.1.call-done) | copy-start | bytes 12582916
Sparse Core Ops, SparseCore 0:
  18.7 60.1 all-gather.1

commit v2 on v1

v2 whole, which is shorter than its diff:
```python
import jax
import jax.numpy as jnp
from jax import lax
from jax.experimental import pallas as pl
from jax.experimental.pallas import tpu as pltpu
from jax.sharding import Mesh, PartitionSpec as P

B = 128
NZ, NX, NY = 8, 4, 4
HIGH = lax.Precision.HIGH


def shift_perm(n, d):
    return [(i, (i + d) % n) for i in range(n)]


def zxy(z, x, y):
    return (z * NX + x) * NY + y


def list_kernel(pattern_ref, y_ref, root_ref, out_ref):
    for m in range(8):
        k = pattern_ref[m] - 8 * y_ref[0]
        ok = jnp.logical_and(k >= 0, k < 8)
        start = pl.multiple_of(jnp.clip(k, 0, 7) * B, B)
        out_ref[m] = jnp.where(ok, root_ref[:, pl.ds(start, B)], 0.0)


def keep_kernel(pattern_ref, cut_ref, out_ref):
    rows = [cut_ref[pattern_ref[j]] for j in range(8)]
    for t in range(NZ):
        for j in range(8):
            out_ref[t, j] = rows[j]


def scalar_spec():
    return pl.BlockSpec(memory_space=pltpu.SMEM)


def vmem_spec():
    return pl.BlockSpec(memory_space=pltpu.VMEM)


def shards(root_inverse, pattern, child_rows, child_inverse):
    z = lax.axis_index("z")
    x = lax.axis_index("x")
    y = lax.axis_index("col")
    f32 = jnp.float32

    listed = pl.pallas_call(
        list_kernel,
        out_shape=jax.ShapeDtypeStruct((8, B, B), f32),
        in_specs=[scalar_spec(), scalar_spec(), vmem_spec()],
        out_specs=vmem_spec(),
    )(pattern, y.astype(jnp.int32).reshape(1), root_inverse)

    def listed_for(target):
        return lax.dynamic_slice_in_dim(listed, 2 * target, 2, axis=0)

    cols = listed_for(y)
    for d in (1, 2, 3):
        pairs = [
            (a * NY + c, a * NY + (c + d) % NY) for a in range(4) for c in range(2)
        ]
        cols = cols + lax.ppermute(
            listed_for(lax.rem(y + d, NY)), ("z", "col"), pairs
        )

    parts = [child_rows] + [
        lax.ppermute(child_rows, "x", shift_perm(NX, d)) for d in (1, 2, 3)
    ]
    block = jnp.zeros((NX, 32, 1024), f32)
    for d in range(NX):
        block = lax.dynamic_update_slice(
            block, parts[d][None], (lax.rem(x + NX - d, NX), 0, 0)
        )
    block = block.reshape(B, 1024)

    e = lax.rem(z, 2)
    high = z // 4
    halves = child_rows.reshape(32, 2, 512)
    places = [(a, b, c) for a in range(NZ) for b in range(NX) for c in range(NY)]
    straight = [
        (zxy(a, b, c), zxy(2 * c + a // 4, b, a % 4)) for a, b, c in places
    ]
    crossed = [
        (zxy(a, b, c), zxy(2 * c + 1 - a // 4, b, a % 4)) for a, b, c in places
    ]
    mine = lax.ppermute(
        lax.dynamic_slice_in_dim(halves, high, 1, axis=1).reshape(32, 512),
        ("z", "x", "col"), straight,
    )
    other = lax.ppermute(
        lax.dynamic_slice_in_dim(halves, 1 - high, 1, axis=1).reshape(32, 512),
        ("z", "x", "col"), crossed,
    )
    pair = jnp.where(e == 0, jnp.stack([mine, other]), jnp.stack([other, mine]))
    strip = jnp.zeros((2, 4, 32, 512), f32)
    for d in range(NY):
        got = pair if d == 0 else lax.ppermute(pair, "col", shift_perm(NY, d))
        strip = lax.dynamic_update_slice(
            strip, got[:, None], (0, lax.rem(y + NY - d, NY), 0, 0)
        )
    strip = strip.reshape(256, 512)

    gathered = jnp.zeros((NZ, B, 1024), f32)

    def place(whole, part, d, column=0):
        return lax.dynamic_update_slice(
            whole, part[None], (lax.rem(z + 2 * NZ - d, NZ), 0, column)
        )

    gathered = place(gathered, block, 0)
    up = down = block
    for step in (1, 2, 3):
        up = lax.ppermute(up, "z", shift_perm(NZ, 1))
        down = lax.ppermute(down, "z", shift_perm(NZ, -1))
        gathered = place(gathered, up, step)
        gathered = place(gathered, down, -step)
    left = lax.ppermute(up[:, :512], "z", shift_perm(NZ, 1))
    right = lax.ppermute(down[:, 512:], "z", shift_perm(NZ, -1))
    gathered = place(gathered, left, 4)
    gathered = place(gathered, right, 4, 512)
    gathered = gathered.reshape(1024, 1024)

    cut = cols.reshape(2, NX, 4, 8, B).transpose(0, 2, 1, 3, 4).reshape(32 * 8, B)
    cut = lax.all_to_all(cut, ("z", "x"), 0, 0, tiled=True).reshape(32, 8, B)
    wide = pl.pallas_call(
        keep_kernel,
        out_shape=jax.ShapeDtypeStruct((NZ, 8, 8, B), f32),
        in_specs=[scalar_spec(), vmem_spec()],
        out_specs=vmem_spec(),
    )(pattern, cut).reshape(NZ * 64, B)
    wide = lax.all_to_all(wide, "z", 0, 0, tiled=True)
    picked = (
        wide.reshape(2, 4, 8, 8, B).transpose(2, 1, 3, 0, 4).reshape(256, 256)
    )
    rows = lax.dynamic_slice_in_dim(picked, z * 32, 32, axis=0)

    share = lax.dot_general(
        picked, strip, (((0,), (0,)), ((), ())), precision=HIGH,
        preferred_element_type=f32,
    ).reshape(256, NX, B)

    def share_of(t):
        return lax.dynamic_slice_in_dim(share, t, 1, axis=1).reshape(256, B)

    total = share_of(x)
    for d in (1, 2, 3):
        total = total + lax.ppermute(
            share_of(lax.rem(x + d, NX)), "x", shift_perm(NX, d)
        )

    both = jnp.concatenate(
        [total, rows.reshape(32, 2, B).transpose(1, 0, 2).reshape(64, B)]
    )
    full = jnp.zeros((NY, 320, B), f32)
    for d in range(NY):
        got = both if d == 0 else lax.ppermute(both, "col", shift_perm(NY, d))
        full = lax.dynamic_update_slice(full, got[None], (lax.rem(y + NY - d, NY), 0, 0))
    product = full[:, :256].reshape(1024, B)
    picked_rows = full[:, 256:].reshape(8, 32, B).transpose(0, 2, 1).reshape(1024, 32)

    last = lax.dot_general(
        jnp.concatenate([product, -picked_rows], axis=1), gathered,
        (((0,), (0,)), ((), ())), precision=HIGH, preferred_element_type=f32,
    )
    return last[B:], child_inverse + last[:B]


def solution(mesh):
    inner = Mesh(mesh.devices.reshape(2, NZ, NX, NY), ("shift", "z", "x", "col"))
    whole = P(("shift", "z", "x"), "col")
    return jax.shard_map(
        shards,
        mesh=inner,
        in_specs=(whole, P("shift"), whole, whole),
        out_specs=(whole, whole),
        check_vma=False,
    )
```

time: 129 us -> 122 us (0.946)
  between operations: 34.5 us -> 1.26 us
  starting transfers between devices: 45.9 us -> 58.8 us
  local copies, waits for them, and re-layouts: 7.32 us -> 16.8 us
  Pallas kernels: 0 us -> 3.56 us
  matrix products: 7.26 us -> 4.26 us
  waiting for transfers between devices: 32.6 us -> 34.6 us
  other arithmetic: 0.21 us -> 1.91 us
    ppermute x5 -> x13, starting transfers between devices: 18.4 us -> 31.3 us  [the longest x3 10.3 us: shards(): lax.ppermute(listed_for(lax.rem(y + d, NY)), ('z', 'col'), pairs)]
    dynamic_update_slice x0 -> x9, local copies, waits for them, and re-layouts: none -> 8.38 us  [place(): lax.dynamic_update_slice(whole, part[None], (lax.rem(z + 2 * NZ - d, NZ),...]
    ppermute x5 -> x13, waiting for transfers between devices: 0.01 us -> 7.74 us  [the longest x3 4.99 us: shards(): up = lax.ppermute(up, 'z', shift_perm(NZ, 1))]
    ppermute x3, waiting for transfers between devices: 3.79 us -> 0.01 us  [shards(): lax.ppermute(child_rows, 'x', shift_perm(NX, d))]
    pallas_call x0 -> x2, Pallas kernels: none -> 3.56 us  [the longest x1 1.92 us: shards(): pl.pallas_call(list_kernel, out_shape=jax.ShapeDtypeStruct((8, B, B), f32...]
    dot_general x2 -> x1, matrix products: 6.62 us -> 3.61 us  [shards(): lax.dot_general(jnp.concatenate([product, -picked_rows], axis=1), gathere...]
    all_to_all x1, starting transfers between devices: 5.3 us -> 7.58 us  [shards(): cut = lax.all_to_all(cut, ('z', 'x'), 0, 0, tiled=True).reshape(32, 8, B)]
    all_to_all x1, waiting for transfers between devices: 10.1 us -> 8.08 us  [shards(): wide = lax.all_to_all(wide, 'z', 0, 0, tiled=True)]
  transfers between devices with their start and end apart: 20 -> 27, of which waited for: 9 -> 11; matrix products, arithmetic and copies ran while one was open for 6% -> 14% of each run, Pallas kernels for 0% -> 3%
where the time goes in v2:
time: 122 us; the launch traced here: 121 us
  starting transfers between devices  58.8 us (48%)
  waiting for transfers between devices  34.6 us (28%)
  local copies, waits for them, and re-layouts  16.8 us (14%)
  matrix products  4.26 us (3%)
  Pallas kernels  3.56 us (3%)
  other arithmetic  1.91 us (2%)
  between operations  1.26 us (1%)
    ppermute x3, starting transfers between devices, shards(): lax.ppermute(listed_for(lax.rem(y + d, NY)), ('z', 'col'), pairs)  10.3 us
    dynamic_update_slice x9, local copies, waits for them, and re-layouts, place(): lax.dynamic_update_slice(whole, part[None], (lax.rem(z + 2 * NZ - d, NZ),...  8.38 us
    all_to_all x1, waiting for transfers between devices, shards(): wide = lax.all_to_all(wide, 'z', 0, 0, tiled=True)  8.08 us
    all_to_all x1, starting transfers between devices, shards(): cut = lax.all_to_all(cut, ('z', 'x'), 0, 0, tiled=True).reshape(32, 8, B)  7.58 us
    all_to_all x1, waiting for transfers between devices, shards(): cut = lax.all_to_all(cut, ('z', 'x'), 0, 0, tiled=True).reshape(32, 8, B)  7.16 us
    ppermute x3, waiting for transfers between devices, shards(): got = both if d == 0 else lax.ppermute(both, 'col', shift_perm(NY, d))  5.95 us
    ppermute x3, starting transfers between devices, shards(): lax.ppermute(child_rows, 'x', shift_perm(NX, d))  5.73 us
    ppermute x3, waiting for transfers between devices, shards(): lax.ppermute(share_of(lax.rem(x + d, NX)), 'x', shift_perm(NX, d))  5.66 us
  transfers between devices with their start and end apart: 27, of which 11 were waited for; matrix products, arithmetic and copies ran while one was open for 14% of the time, Pallas kernels for 3%

profile of v2, /device:TPU:8, one launch (start us, length us, event | category | flops | bytes accessed | tf_op | source)
XLA Modules:
  0.0 121.2 jit_solution(5980140569661627719)
XLA Ops:
  0.6 1.6 %collective-permute-start.14 = (f32[32,1024]{1,0:T(8,128)}, f32[32,1024]{1,0:T(8,128)S(1)}, u32[]{:S(2)}, u32[]{:S(2)}) collective-permute-start(f32[32,1024]{1,0:T(8,128)} %param.6), channel_id=1, source_target_pairs={{0,4},{4,8},{8,12},{12,0},{1,5},{5,9},{9,13},{13,1},{2,6},{6,10},{... | collective-permute-start | bytes 393224 | tf_op jit(solution)/shard_map/ppermute | solution.py:70
  2.2 2.7 %collective-permute-start.15 = (f32[32,1024]{1,0:T(8,128)}, f32[32,1024]{1,0:T(8,128)S(1)}, u32[]{:S(2)}, u32[]{:S(2)}) collective-permute-start(f32[32,1024]{1,0:T(8,128)} %param.6), channel_id=1, source_target_pairs={{0,8},{4,12},{8,0},{12,4},{1,9},{5,13},{9,1},{13,5},{2,10},{6,14},... | collective-permute-start | bytes 393224 | tf_op jit(solution)/shard_map/ppermute | solution.py:70
  4.9 1.4 %collective-permute-start.16 = (f32[32,1024]{1,0:T(8,128)}, f32[32,1024]{1,0:T(8,128)S(1)}, u32[]{:S(2)}, u32[]{:S(2)}) collective-permute-start(f32[32,1024]{1,0:T(8,128)} %param.6), channel_id=1, source_target_pairs={{0,12},{4,0},{8,4},{12,8},{1,13},{5,1},{9,5},{13,9},{2,14},{6,2},{... | collective-permute-start | bytes 393224 | tf_op jit(solution)/shard_map/ppermute | solution.py:70
  7.6 4.6 %collective-permute-start.4 = (f32[32,512]{1,0:T(8,128)S(1)}, f32[32,512]{1,0:T(8,128)S(1)}, u32[]{:S(2)}, u32[]{:S(2)}) collective-permute-start(f32[32,512]{1,0:T(8,128)S(1)} %bitcast.118), channel_id=1, source_target_pairs={{0,16},{1,48},{2,80},{3,112},{4,20},{5,52},{6,84},{7,116},{8,24},{... | collective-permute-start | bytes 196616 | tf_op jit(solution)/shard_map/ppermute | solution.py:93
  12.2 3.3 %collective-permute-start.3 = (f32[32,512]{1,0:T(8,128)S(1)}, f32[32,512]{1,0:T(8,128)S(1)}, u32[]{:S(2)}, u32[]{:S(2)}) collective-permute-start(f32[32,512]{1,0:T(8,128)S(1)} %bitcast.117), channel_id=1, source_target_pairs={{0,0},{1,32},{2,64},{3,96},{4,4},{5,36},{6,68},{7,100},{8,8},{9,40... | collective-permute-start | bytes 196616 | tf_op jit(solution)/shard_map/ppermute | solution.py:89
  16.6 1.9 %shard_map.59 = f32[8,128,128]{2,1,0:T(8,128)} custom-call(s32[8]{0:T(128)} %pattern_ref.3, s32[1]{0:T(128)} %bitcast.y_ref, f32[128,1024]{1,0:T(8,128)} %root_ref.1), custom_call_target="tpu_custom_call" | custom-call | tf_op jit(solution)/shard_map/pallas_call | solution.py:50
  19.6 1.3 %collective-permute-start.2 = (f32[2,128,128]{2,1,0:T(8,128)S(1)}, f32[2,128,128]{2,1,0:T(8,128)S(1)}, u32[]{:S(2)}, u32[]{:S(2)}) collective-permute-start(f32[2,128,128]{2,1,0:T(8,128)S(1)} %get-tuple-element.6), channel_id=1, source_target_pairs={{0,3},{1,0},{16,19},{17,16},{32,35},{33,32},{48,51},{49,48},{4,7},... | collective-permute-start | bytes 393224 | tf_op jit(solution)/shard_map/ppermute | solution.py:65
  20.9 7.1 %collective-permute-start.1 = (f32[2,128,128]{2,1,0:T(8,128)S(1)}, f32[2,128,128]{2,1,0:T(8,128)S(1)}, u32[]{:S(2)}, u32[]{:S(2)}) collective-permute-start(f32[2,128,128]{2,1,0:T(8,128)S(1)} %get-tuple-element.7), channel_id=1, source_target_pairs={{0,2},{1,3},{16,18},{17,19},{32,34},{33,35},{48,50},{49,51},{4,6},... | collective-permute-start | bytes 393224 | tf_op jit(solution)/shard_map/ppermute | solution.py:65
  28.1 1.9 %collective-permute-start = (f32[2,128,128]{2,1,0:T(8,128)S(1)}, f32[2,128,128]{2,1,0:T(8,128)S(1)}, u32[]{:S(2)}, u32[]{:S(2)}) collective-permute-start(f32[2,128,128]{2,1,0:T(8,128)S(1)} %get-tuple-element.5), channel_id=1, source_target_pairs={{0,1},{1,2},{16,17},{17,18},{32,33},{33,34},{48,49},{49,50},{4,5},... | collective-permute-start | bytes 393224 | tf_op jit(solution)/shard_map/ppermute | solution.py:65
  30.2 4.2 %collective-permute-start.6 = (f32[2,32,512]{2,1,0:T(8,128)S(1)}, f32[2,32,512]{2,1,0:T(8,128)S(1)}, u32[]{:S(2)}, u32[]{:S(2)}) collective-permute-start(f32[2,32,512]{2,1,0:T(8,128)S(1)} %maximum_select_fusion.1), channel_id=1, source_target_pairs={{0,2},{1,3},{2,0},{3,1},{4,6},{5,7},{6,4},{7,5},{8,10},{9,11},{10,... | collective-permute-start | bytes 393224 | tf_op jit(solution)/shard_map/ppermute | solution.py:100
  34.5 2.3 %collective-permute-start.17 = (f32[128,1024]{1,0:T(8,128)S(1)}, f32[128,1024]{1,0:T(8,128)S(1)}, u32[]{:S(2)}, u32[]{:S(2)}) collective-permute-start(f32[128,1024]{1,0:T(8,128)S(1)} %bitcast.101), channel_id=1, source_target_pairs={{0,16},{16,32},{32,48},{48,64},{64,80},{80,96},{96,112},{112,0},{1... | collective-permute-start | bytes 1572872 | tf_op jit(solution)/shard_map/ppermute | solution.py:116
  39.4 7.6 %all-to-all-start = ((f32[32,8,128]{2,1,0:T(8,128)}), f32[32,8,128]{2,1,0:T(8,128)S(1)}, u32[]{:S(2)}, u32[]{:S(2)}) async-start(f32[32,8,128]{2,1,0:T(8,128)} %bitcast.3), calls=%async_computation | async-start | bytes 262144 | tf_op jit(solution)/shard_map/all_to_all | solution.py:127
  47.0 2.5 %broadcast_in_dim.79 = f32[8,128,1024]{2,1,0:T(8,128)} broadcast(f32[]{:T(128)} %constant.109.clone.1), dimensions={} | broadcast | bytes 4194308 | tf_op jit(solution)/shard_map/broadcast_in_dim | solution.py:106
  50.3 7.2 %all-to-all-done.cut_ref = f32[32,8,128]{2,1,0:T(8,128)S(1)} async-done(((f32[32,8,128]{2,1,0:T(8,128)}), f32[32,8,128]{2,1,0:T(8,128)S(1)}, u32[]{:S(2)}, u32[]{:S(2)}) %all-to-all-start) | async-done | bytes 131104 | tf_op jit(solution)/shard_map/all_to_all | solution.py:127
  58.2 1.6 %shard_map.60 = f32[8,8,8,128]{3,2,1,0:T(8,128)} custom-call(s32[8]{0:T(128)} %pattern_ref.3, f32[32,8,128]{2,1,0:T(8,128)} %copy-done.1), custom_call_target="tpu_custom_call" | custom-call | tf_op jit(solution)/shard_map/pallas_call | solution.py:128
  59.8 3.4 %all-to-all-start.1 = ((f32[8,64,128]{2,1,0:T(8,128)}), f32[8,64,128]{2,1,0:T(8,128)S(1)}, u32[]{:S(2)}, u32[]{:S(2)}) async-start(f32[8,64,128]{2,1,0:T(8,128)} %bitcast.107), calls=%async_computation.1 | async-start | bytes 524288 | tf_op jit(solution)/shard_map/all_to_all | solution.py:134
  63.5 2.0 %collective-permute-start.19 = (f32[128,1024]{1,0:T(8,128)S(1)}, f32[128,1024]{1,0:T(8,128)}, u32[]{:S(2)}, u32[]{:S(2)}) collective-permute-start(f32[128,1024]{1,0:T(8,128)S(1)} %collective-permute-done.17), channel_id=1, source_target_pairs={{0,16},{16,32},{32,48},{48,64},{64,80},{80,96},{96,112},{112,0},{1... | collective-permute-start | bytes 1572872 | tf_op jit(solution)/shard_map/ppermute | solution.py:116
  65.5 1.3 %collective-permute-start.20 = (f32[128,1024]{1,0:T(8,128)S(1)}, f32[128,1024]{1,0:T(8,128)S(1)}, u32[]{:S(2)}, u32[]{:S(2)}) collective-permute-start(f32[128,1024]{1,0:T(8,128)S(1)} %collective-permute-done.18), channel_id=1, source_target_pairs={{0,112},{16,0},{32,16},{48,32},{64,48},{80,64},{96,80},{112,96},{1... | collective-permute-start | bytes 1572872 | tf_op jit(solution)/shard_map/ppermute | solution.py:117
  66.8 8.1 %all-to-all-done.1 = f32[8,64,128]{2,1,0:T(8,128)S(1)} async-done(((f32[8,64,128]{2,1,0:T(8,128)}), f32[8,64,128]{2,1,0:T(8,128)S(1)}, u32[]{:S(2)}, u32[]{:S(2)}) %all-to-all-start.1) | async-done | bytes 262176 | tf_op jit(solution)/shard_map/all_to_all | solution.py:134
  75.6 1.4 %collective-permute-start.10 = (f32[256,128]{1,0:T(8,128)S(1)}, f32[256,128]{1,0:T(8,128)S(1)}, u32[]{:S(2)}, u32[]{:S(2)}) collective-permute-start(f32[256,128]{1,0:T(8,128)S(1)} %get-tuple-element.3), channel_id=1, source_target_pairs={{0,12},{4,0},{8,4},{12,8},{1,13},{5,1},{9,5},{13,9},{2,14},{6,2},{... | collective-permute-start | bytes 393224 | tf_op jit(solution)/shard_map/ppermute | solution.py:150
  79.2 1.5 %collective-permute-done.10 = f32[256,128]{1,0:T(8,128)S(1)} collective-permute-done((f32[256,128]{1,0:T(8,128)S(1)}, f32[256,128]{1,0:T(8,128)S(1)}, u32[]{:S(2)}, u32[]{:S(2)}) %collective-permute-start.10) | collective-permute-done | bytes 131104 | tf_op jit(solution)/shard_map/ppermute | solution.py:150
  80.7 2.9 %collective-permute-done.9 = f32[256,128]{1,0:T(8,128)S(1)} collective-permute-done((f32[256,128]{1,0:T(8,128)S(1)}, f32[256,128]{1,0:T(8,128)S(1)}, u32[]{:S(2)}, u32[]{:S(2)}) %collective-permute-start.9) | collective-permute-done | bytes 131104 | tf_op jit(solution)/shard_map/ppermute | solution.py:150
  83.6 1.3 %collective-permute-done.8 = f32[256,128]{1,0:T(8,128)S(1)} collective-permute-done((f32[256,128]{1,0:T(8,128)S(1)}, f32[256,128]{1,0:T(8,128)S(1)}, u32[]{:S(2)}, u32[]{:S(2)}) %collective-permute-start.8) | collective-permute-done | bytes 131104 | tf_op jit(solution)/shard_map/ppermute | solution.py:150
  84.9 1.6 %collective-permute-start.11 = (f32[320,128]{1,0:T(8,128)S(1)}, f32[320,128]{1,0:T(8,128)S(1)}, u32[]{:S(2)}, u32[]{:S(2)}) collective-permute-start(f32[320,128]{1,0:T(8,128)S(1)} %pad_maximum_fusion), channel_id=1, source_target_pairs={{0,1},{1,2},{2,3},{3,0},{4,5},{5,6},{6,7},{7,4},{8,9},{9,10},{10,1... | collective-permute-start | bytes 491528 | tf_op jit(solution)/shard_map/ppermute | solution.py:159
  90.4 4.0 %collective-permute-done.12 = f32[320,128]{1,0:T(8,128)S(1)} collective-permute-done((f32[320,128]{1,0:T(8,128)S(1)}, f32[320,128]{1,0:T(8,128)S(1)}, u32[]{:S(2)}, u32[]{:S(2)}) %collective-permute-start.12) | collective-permute-done | bytes 163872 | tf_op jit(solution)/shard_map/ppermute | solution.py:159
  94.4 1.2 collective-permute-done.13
  96.2 2.7 %collective-permute-start.22 = (f32[128,1024]{1,0:T(8,128)S(1)}, f32[128,1024]{1,0:T(8,128)S(1)}, u32[]{:S(2)}, u32[]{:S(2)}) collective-permute-start(f32[128,1024]{1,0:T(8,128)S(1)} %collective-permute-done.20), channel_id=1, source_target_pairs={{0,112},{16,0},{32,16},{48,32},{64,48},{80,64},{96,80},{112,96},{1... | collective-permute-start | bytes 1572872 | tf_op jit(solution)/shard_map/ppermute | solution.py:117
  99.2 1.9 %bitcast_dynamic-update-slice_fusion.3 = f32[8,128,1024]{2,1,0:T(8,128)} fusion(f32[8,128,1024]{2,1,0:T(8,128)} %bitcast_dynamic-update-slice_fusion.4, s32[]{:T(128)S(6)} %select_n.128, f32[128,1024]{1,0:T(8,128)} %collective-permute-done.19), kind=kLoop, calls=%fused_computation.8 | loop fusion | bytes 1048580 | tf_op jit(solution)/shard_map/dynamic_update_slice | solution.py:109
  101.9 5.0 %collective-permute-done.21 = f32[128,1024]{1,0:T(8,128)S(1)} collective-permute-done((f32[128,1024]{1,0:T(8,128)}, f32[128,1024]{1,0:T(8,128)S(1)}, u32[]{:S(2)}, u32[]{:S(2)}) %collective-permute-start.21) | collective-permute-done | bytes 524320 | tf_op jit(solution)/shard_map/ppermute | solution.py:116
  107.0 3.3 %collective-permute-start.24 = (f32[128,512]{1,0:T(8,128)S(1)}, f32[128,512]{1,0:T(8,128)S(1)}, u32[]{:S(2)}, u32[]{:S(2)}) collective-permute-start(f32[128,512]{1,0:T(8,128)S(1)} %slice.27), channel_id=1, source_target_pairs={{0,112},{16,0},{32,16},{48,32},{64,48},{80,64},{96,80},{112,96},{1... | collective-permute-start | bytes 786440 | tf_op jit(solution)/shard_map/ppermute | solution.py:121
  112.0 2.6 %collective-permute-done.23 = f32[128,512]{1,0:T(8,128)S(1)} collective-permute-done((f32[128,512]{1,0:T(8,128)S(1)}, f32[128,512]{1,0:T(8,128)S(1)}, u32[]{:S(2)}, u32[]{:S(2)}) %collective-permute-start.23) | collective-permute-done | bytes 262176 | tf_op jit(solution)/shard_map/ppermute | solution.py:120
  116.1 3.6 %fusion = f32[160,1024]{1,0:T(8,128)S(1)} fusion(f32[1024,1024]{1,0:T(8,128)} %bitcast.52, f32[1024,32]{1,0:T(8,128)S(1)} %bitcast.97, f32[1024,128]{1,0:T(8,128)S(1)} %bitcast.98), kind=kOutput, calls=%fused_computation | convolution fusion | flops 1006796800 | bytes 5505024 | tf_op jit(solution)/shard_map/dot_general | solution.py:164
  (78 shorter events, 21.2 us)
Async XLA Ops:
  0.6 27.5 %collective-permute-start.14 = (f32[32,1024]{1,0:T(8,128)}, f32[32,1024]{1,0:T(8,128)S(1)}, u32[]{:S(2)}, u32[]{:S(2)}) collective-permute-start(f32[32,1024]{1,0:T(8,128)} %param.6), channel_id=1, source_target_pairs={{0,4},{4,8},{8,12},{12,0},{1,5},{5,9},{9,13},{13,1},{2,6},{6,10},{... | collective-permute-start | bytes 393224 | tf_op jit(solution)/shard_map/ppermute | solution.py:70
  2.2 27.9 %collective-permute-start.15 = (f32[32,1024]{1,0:T(8,128)}, f32[32,1024]{1,0:T(8,128)S(1)}, u32[]{:S(2)}, u32[]{:S(2)}) collective-permute-start(f32[32,1024]{1,0:T(8,128)} %param.6), channel_id=1, source_target_pairs={{0,8},{4,12},{8,0},{12,4},{1,9},{5,13},{9,1},{13,5},{2,10},{6,14},... | collective-permute-start | bytes 393224 | tf_op jit(solution)/shard_map/ppermute | solution.py:70
  4.9 25.3 %collective-permute-start.16 = (f32[32,1024]{1,0:T(8,128)}, f32[32,1024]{1,0:T(8,128)S(1)}, u32[]{:S(2)}, u32[]{:S(2)}) collective-permute-start(f32[32,1024]{1,0:T(8,128)} %param.6), channel_id=1, source_target_pairs={{0,12},{4,0},{8,4},{12,8},{1,13},{5,1},{9,5},{13,9},{2,14},{6,2},{... | collective-permute-start | bytes 393224 | tf_op jit(solution)/shard_map/ppermute | solution.py:70
  7.6 12.0 %collective-permute-start.4 = (f32[32,512]{1,0:T(8,128)S(1)}, f32[32,512]{1,0:T(8,128)S(1)}, u32[]{:S(2)}, u32[]{:S(2)}) collective-permute-start(f32[32,512]{1,0:T(8,128)S(1)} %bitcast.118), channel_id=1, source_target_pairs={{0,16},{1,48},{2,80},{3,112},{4,20},{5,52},{6,84},{7,116},{8,24},{... | collective-permute-start | bytes 196616 | tf_op jit(solution)/shard_map/ppermute | solution.py:93
  12.2 8.8 %collective-permute-start.3 = (f32[32,512]{1,0:T(8,128)S(1)}, f32[32,512]{1,0:T(8,128)S(1)}, u32[]{:S(2)}, u32[]{:S(2)}) collective-permute-start(f32[32,512]{1,0:T(8,128)S(1)} %bitcast.117), channel_id=1, source_target_pairs={{0,0},{1,32},{2,64},{3,96},{4,4},{5,36},{6,68},{7,100},{8,8},{9,40... | collective-permute-start | bytes 196616 | tf_op jit(solution)/shard_map/ppermute | solution.py:89
  19.6 14.8 %collective-permute-start.2 = (f32[2,128,128]{2,1,0:T(8,128)S(1)}, f32[2,128,128]{2,1,0:T(8,128)S(1)}, u32[]{:S(2)}, u32[]{:S(2)}) collective-permute-start(f32[2,128,128]{2,1,0:T(8,128)S(1)} %get-tuple-element.6), channel_id=1, source_target_pairs={{0,3},{1,0},{16,19},{17,16},{32,35},{33,32},{48,51},{49,48},{4,7},... | collective-permute-start | bytes 393224 | tf_op jit(solution)/shard_map/ppermute | solution.py:65
  20.9 13.5 %collective-permute-start.1 = (f32[2,128,128]{2,1,0:T(8,128)S(1)}, f32[2,128,128]{2,1,0:T(8,128)S(1)}, u32[]{:S(2)}, u32[]{:S(2)}) collective-permute-start(f32[2,128,128]{2,1,0:T(8,128)S(1)} %get-tuple-element.7), channel_id=1, source_target_pairs={{0,2},{1,3},{16,18},{17,19},{32,34},{33,35},{48,50},{49,51},{4,6},... | collective-permute-start | bytes 393224 | tf_op jit(solution)/shard_map/ppermute | solution.py:65
  28.1 8.8 %collective-permute-start = (f32[2,128,128]{2,1,0:T(8,128)S(1)}, f32[2,128,128]{2,1,0:T(8,128)S(1)}, u32[]{:S(2)}, u32[]{:S(2)}) collective-permute-start(f32[2,128,128]{2,1,0:T(8,128)S(1)} %get-tuple-element.5), channel_id=1, source_target_pairs={{0,1},{1,2},{16,17},{17,18},{32,33},{33,34},{48,49},{49,50},{4,5},... | collective-permute-start | bytes 393224 | tf_op jit(solution)/shard_map/ppermute | solution.py:65
  30.1 20.2 %collective-permute-start.5 = (f32[2,32,512]{2,1,0:T(8,128)S(1)}, f32[2,32,512]{2,1,0:T(8,128)S(1)}, u32[]{:S(2)}, u32[]{:S(2)}) collective-permute-start(f32[2,32,512]{2,1,0:T(8,128)S(1)} %maximum_select_fusion.1), channel_id=1, source_target_pairs={{0,1},{1,2},{2,3},{3,0},{4,5},{5,6},{6,7},{7,4},{8,9},{9,10},{10,1... | collective-permute-start | bytes 393224 | tf_op jit(solution)/shard_map/ppermute | solution.py:100
  30.2 33.0 %collective-permute-start.6 = (f32[2,32,512]{2,1,0:T(8,128)S(1)}, f32[2,32,512]{2,1,0:T(8,128)S(1)}, u32[]{:S(2)}, u32[]{:S(2)}) collective-permute-start(f32[2,32,512]{2,1,0:T(8,128)S(1)} %maximum_select_fusion.1), channel_id=1, source_target_pairs={{0,2},{1,3},{2,0},{3,1},{4,6},{5,7},{6,4},{7,5},{8,10},{9,11},{10,... | collective-permute-start | bytes 393224 | tf_op jit(solution)/shard_map/ppermute | solution.py:100
  34.4 28.9 %collective-permute-start.7 = (f32[2,32,512]{2,1,0:T(8,128)S(1)}, f32[2,32,512]{2,1,0:T(8,128)S(1)}, u32[]{:S(2)}, u32[]{:S(2)}) collective-permute-start(f32[2,32,512]{2,1,0:T(8,128)S(1)} %maximum_select_fusion.1), channel_id=1, source_target_pairs={{0,3},{1,0},{2,1},{3,2},{4,7},{5,4},{6,5},{7,6},{8,11},{9,8},{10,9... | collective-permute-start | bytes 393224 | tf_op jit(solution)/shard_map/ppermute | solution.py:100
  34.5 29.0 %collective-permute-start.17 = (f32[128,1024]{1,0:T(8,128)S(1)}, f32[128,1024]{1,0:T(8,128)S(1)}, u32[]{:S(2)}, u32[]{:S(2)}) collective-permute-start(f32[128,1024]{1,0:T(8,128)S(1)} %bitcast.101), channel_id=1, source_target_pairs={{0,16},{16,32},{32,48},{48,64},{64,80},{80,96},{96,112},{112,0},{1... | collective-permute-start | bytes 1572872 | tf_op jit(solution)/shard_map/ppermute | solution.py:116
  36.9 28.6 %collective-permute-start.18 = (f32[128,1024]{1,0:T(8,128)S(1)}, f32[128,1024]{1,0:T(8,128)S(1)}, u32[]{:S(2)}, u32[]{:S(2)}) collective-permute-start(f32[128,1024]{1,0:T(8,128)S(1)} %bitcast.102), channel_id=1, source_target_pairs={{0,112},{16,0},{32,16},{48,32},{64,48},{80,64},{96,80},{112,96},{1... | collective-permute-start | bytes 1572872 | tf_op jit(solution)/shard_map/ppermute | solution.py:117
  39.4 18.1 %all-to-all-start = ((f32[32,8,128]{2,1,0:T(8,128)}), f32[32,8,128]{2,1,0:T(8,128)S(1)}, u32[]{:S(2)}, u32[]{:S(2)}) async-start(f32[32,8,128]{2,1,0:T(8,128)} %bitcast.3), calls=%async_computation | async-start | bytes 262144 | tf_op jit(solution)/shard_map/all_to_all | solution.py:127
  57.5 0.7 copy-start.1
  59.8 15.1 %all-to-all-start.1 = ((f32[8,64,128]{2,1,0:T(8,128)}), f32[8,64,128]{2,1,0:T(8,128)S(1)}, u32[]{:S(2)}, u32[]{:S(2)}) async-start(f32[8,64,128]{2,1,0:T(8,128)} %bitcast.107), calls=%async_computation.1 | async-start | bytes 524288 | tf_op jit(solution)/shard_map/all_to_all | solution.py:134
  63.5 32.1 %collective-permute-start.19 = (f32[128,1024]{1,0:T(8,128)S(1)}, f32[128,1024]{1,0:T(8,128)}, u32[]{:S(2)}, u32[]{:S(2)}) collective-permute-start(f32[128,1024]{1,0:T(8,128)S(1)} %collective-permute-done.17), channel_id=1, source_target_pairs={{0,16},{16,32},{32,48},{48,64},{64,80},{80,96},{96,112},{112,0},{1... | collective-permute-start | bytes 1572872 | tf_op jit(solution)/shard_map/ppermute | solution.py:116
  65.5 30.8 %collective-permute-start.20 = (f32[128,1024]{1,0:T(8,128)S(1)}, f32[128,1024]{1,0:T(8,128)S(1)}, u32[]{:S(2)}, u32[]{:S(2)}) collective-permute-start(f32[128,1024]{1,0:T(8,128)S(1)} %collective-permute-done.18), channel_id=1, source_target_pairs={{0,112},{16,0},{32,16},{48,32},{64,48},{80,64},{96,80},{112,96},{1... | collective-permute-start | bytes 1572872 | tf_op jit(solution)/shard_map/ppermute | solution.py:117
  75.6 5.0 %collective-permute-start.10 = (f32[256,128]{1,0:T(8,128)S(1)}, f32[256,128]{1,0:T(8,128)S(1)}, u32[]{:S(2)}, u32[]{:S(2)}) collective-permute-start(f32[256,128]{1,0:T(8,128)S(1)} %get-tuple-element.3), channel_id=1, source_target_pairs={{0,12},{4,0},{8,4},{12,8},{1,13},{5,1},{9,5},{13,9},{2,14},{6,2},{... | collective-permute-start | bytes 393224 | tf_op jit(solution)/shard_map/ppermute | solution.py:150
  77.0 6.5 %collective-permute-start.9 = (f32[256,128]{1,0:T(8,128)S(1)}, f32[256,128]{1,0:T(8,128)S(1)}, u32[]{:S(2)}, u32[]{:S(2)}) collective-permute-start(f32[256,128]{1,0:T(8,128)S(1)} %get-tuple-element.4), channel_id=1, source_target_pairs={{0,8},{4,12},{8,0},{12,4},{1,9},{5,13},{9,1},{13,5},{2,10},{6,14},... | collective-permute-start | bytes 393224 | tf_op jit(solution)/shard_map/ppermute | solution.py:150
  78.0 6.9 %collective-permute-start.8 = (f32[256,128]{1,0:T(8,128)S(1)}, f32[256,128]{1,0:T(8,128)S(1)}, u32[]{:S(2)}, u32[]{:S(2)}) collective-permute-start(f32[256,128]{1,0:T(8,128)S(1)} %get-tuple-element.2), channel_id=1, source_target_pairs={{0,4},{4,8},{8,12},{12,0},{1,5},{5,9},{9,13},{13,1},{2,6},{6,10},{... | collective-permute-start | bytes 393224 | tf_op jit(solution)/shard_map/ppermute | solution.py:150
  84.9 5.4 %collective-permute-start.11 = (f32[320,128]{1,0:T(8,128)S(1)}, f32[320,128]{1,0:T(8,128)S(1)}, u32[]{:S(2)}, u32[]{:S(2)}) collective-permute-start(f32[320,128]{1,0:T(8,128)S(1)} %pad_maximum_fusion), channel_id=1, source_target_pairs={{0,1},{1,2},{2,3},{3,0},{4,5},{5,6},{6,7},{7,4},{8,9},{9,10},{10,1... | collective-permute-start | bytes 491528 | tf_op jit(solution)/shard_map/ppermute | solution.py:159
  87.4 6.9 %collective-permute-start.12 = (f32[320,128]{1,0:T(8,128)S(1)}, f32[320,128]{1,0:T(8,128)S(1)}, u32[]{:S(2)}, u32[]{:S(2)}) collective-permute-start(f32[320,128]{1,0:T(8,128)S(1)} %pad_maximum_fusion), channel_id=1, source_target_pairs={{0,2},{1,3},{2,0},{3,1},{4,6},{5,7},{6,4},{7,5},{8,10},{9,11},{10,... | collective-permute-start | bytes 491528 | tf_op jit(solution)/shard_map/ppermute | solution.py:159
  88.5 7.1 %collective-permute-start.13 = (f32[320,128]{1,0:T(8,128)S(1)}, f32[320,128]{1,0:T(8,128)S(1)}, u32[]{:S(2)}, u32[]{:S(2)}) collective-permute-start(f32[320,128]{1,0:T(8,128)S(1)} %pad_maximum_fusion), channel_id=1, source_target_pairs={{0,3},{1,0},{2,1},{3,2},{4,7},{5,4},{6,5},{7,6},{8,11},{9,8},{10,9... | collective-permute-start | bytes 491528 | tf_op jit(solution)/shard_map/ppermute | solution.py:159
  95.6 11.3 %collective-permute-start.21 = (f32[128,1024]{1,0:T(8,128)}, f32[128,1024]{1,0:T(8,128)S(1)}, u32[]{:S(2)}, u32[]{:S(2)}) collective-permute-start(f32[128,1024]{1,0:T(8,128)} %collective-permute-done.19), channel_id=1, source_target_pairs={{0,16},{16,32},{32,48},{48,64},{64,80},{80,96},{96,112},{112,0},{1... | collective-permute-start | bytes 1572872 | tf_op jit(solution)/shard_map/ppermute | solution.py:116
  96.2 10.8 %collective-permute-start.22 = (f32[128,1024]{1,0:T(8,128)S(1)}, f32[128,1024]{1,0:T(8,128)S(1)}, u32[]{:S(2)}, u32[]{:S(2)}) collective-permute-start(f32[128,1024]{1,0:T(8,128)S(1)} %collective-permute-done.20), channel_id=1, source_target_pairs={{0,112},{16,0},{32,16},{48,32},{64,48},{80,64},{96,80},{112,96},{1... | collective-permute-start | bytes 1572872 | tf_op jit(solution)/shard_map/ppermute | solution.py:117
  106.9 7.7 %collective-permute-start.23 = (f32[128,512]{1,0:T(8,128)S(1)}, f32[128,512]{1,0:T(8,128)S(1)}, u32[]{:S(2)}, u32[]{:S(2)}) collective-permute-start(f32[128,512]{1,0:T(8,128)S(1)} %slice.26), channel_id=1, source_target_pairs={{0,16},{16,32},{32,48},{48,64},{64,80},{80,96},{96,112},{112,0},{1... | collective-permute-start | bytes 786440 | tf_op jit(solution)/shard_map/ppermute | solution.py:120
  107.0 8.3 %collective-permute-start.24 = (f32[128,512]{1,0:T(8,128)S(1)}, f32[128,512]{1,0:T(8,128)S(1)}, u32[]{:S(2)}, u32[]{:S(2)}) collective-permute-start(f32[128,512]{1,0:T(8,128)S(1)} %slice.27), channel_id=1, source_target_pairs={{0,112},{16,0},{32,16},{48,32},{64,48},{80,64},{96,80},{112,96},{1... | collective-permute-start | bytes 786440 | tf_op jit(solution)/shard_map/ppermute | solution.py:121
  111.2 9.2 %copy-start = (f32[128,1024]{1,0:T(8,128)S(1)}, f32[128,1024]{1,0:T(8,128)}, u32[]{:S(2)}) copy-start(f32[128,1024]{1,0:T(8,128)} %param.7) | copy-start | bytes 1572868

commit v3 on v2

--- a/solution.py
+++ b/solution.py
@@ -14,20 +14,25 @@
     return [(i, (i + d) % n) for i in range(n)]
 
 
+def after(value, *done):
+    return lax.optimization_barrier((value, *done))[0]
+
+
 def zxy(z, x, y):
     return (z * NX + x) * NY + y
 
 
 def list_kernel(pattern_ref, y_ref, root_ref, out_ref):
     for m in range(8):
-        k = pattern_ref[m] - 8 * y_ref[0]
-        ok = jnp.logical_and(k >= 0, k < 8)
-        start = pl.multiple_of(jnp.clip(k, 0, 7) * B, B)
-        out_ref[m] = jnp.where(ok, root_ref[:, pl.ds(start, B)], 0.0)
+        k = jnp.clip(pattern_ref[m] - 8 * y_ref[0], 0, 7)
+        column = root_ref[:, pl.ds(pl.multiple_of(k * B, B), B)]
+        for row in range(16):
+            out_ref[m % 2, row % 4, row // 4, m // 2] = column[8 * row : 8 * row + 8]
 
 
-def keep_kernel(pattern_ref, cut_ref, out_ref):
-    rows = [cut_ref[pattern_ref[j]] for j in range(8)]
+def keep_kernel(pattern_ref, m_ref, cut_ref, out_ref):
+    owner = pattern_ref[m_ref[0]] // 8
+    rows = [cut_ref[pattern_ref[j] * NY + owner] for j in range(8)]
     for t in range(NZ):
         for j in range(8):
             out_ref[t, j] = rows[j]
@@ -47,25 +52,6 @@
     y = lax.axis_index("col")
     f32 = jnp.float32
 
-    listed = pl.pallas_call(
-        list_kernel,
-        out_shape=jax.ShapeDtypeStruct((8, B, B), f32),
-        in_specs=[scalar_spec(), scalar_spec(), vmem_spec()],
-        out_specs=vmem_spec(),
-    )(pattern, y.astype(jnp.int32).reshape(1), root_inverse)
-
-    def listed_for(target):
-        return lax.dynamic_slice_in_dim(listed, 2 * target, 2, axis=0)
-
-    cols = listed_for(y)
-    for d in (1, 2, 3):
-        pairs = [
-            (a * NY + c, a * NY + (c + d) % NY) for a in range(4) for c in range(2)
-        ]
-        cols = cols + lax.ppermute(
-            listed_for(lax.rem(y + d, NY)), ("z", "col"), pairs
-        )
-
     parts = [child_rows] + [
         lax.ppermute(child_rows, "x", shift_perm(NX, d)) for d in (1, 2, 3)
     ]
@@ -78,7 +64,7 @@
 
     e = lax.rem(z, 2)
     high = z // 4
-    halves = child_rows.reshape(32, 2, 512)
+    halves = after(child_rows, block).reshape(32, 2, 512)
     places = [(a, b, c) for a in range(NZ) for b in range(NX) for c in range(NY)]
     straight = [
         (zxy(a, b, c), zxy(2 * c + a // 4, b, a % 4)) for a, b, c in places
@@ -112,9 +98,11 @@
 
     gathered = place(gathered, block, 0)
     up = down = block
+    ring = []
     for step in (1, 2, 3):
         up = lax.ppermute(up, "z", shift_perm(NZ, 1))
         down = lax.ppermute(down, "z", shift_perm(NZ, -1))
+        ring.append((up, down))
         gathered = place(gathered, up, step)
         gathered = place(gathered, down, -step)
     left = lax.ppermute(up[:, :512], "z", shift_perm(NZ, 1))
@@ -123,14 +111,21 @@
     gathered = place(gathered, right, 4, 512)
     gathered = gathered.reshape(1024, 1024)
 
-    cut = cols.reshape(2, NX, 4, 8, B).transpose(0, 2, 1, 3, 4).reshape(32 * 8, B)
-    cut = lax.all_to_all(cut, ("z", "x"), 0, 0, tiled=True).reshape(32, 8, B)
+    listed = pl.pallas_call(
+        list_kernel,
+        out_shape=jax.ShapeDtypeStruct((2, 4, NX, NY, 8, B), f32),
+        in_specs=[scalar_spec(), scalar_spec(), vmem_spec()],
+        out_specs=vmem_spec(),
+    )(pattern, y.astype(jnp.int32).reshape(1), root_inverse)
+    listed = after(listed.reshape(128 * 8, B), block)
+    cut = lax.all_to_all(listed, ("z", "x", "col"), 0, 0, tiled=True)
     wide = pl.pallas_call(
         keep_kernel,
         out_shape=jax.ShapeDtypeStruct((NZ, 8, 8, B), f32),
-        in_specs=[scalar_spec(), vmem_spec()],
+        in_specs=[scalar_spec(), scalar_spec(), vmem_spec()],
         out_specs=vmem_spec(),
-    )(pattern, cut).reshape(NZ * 64, B)
+    )(pattern, (2 * y + high).astype(jnp.int32).reshape(1), cut.reshape(128, 8, B))
+    wide = after(wide.reshape(NZ * 64, B), *ring[0])
     wide = lax.all_to_all(wide, "z", 0, 0, tiled=True)
     picked = (
         wide.reshape(2, 4, 8, 8, B).transpose(2, 1, 3, 0, 4).reshape(256, 256)
@@ -141,6 +136,7 @@
         picked, strip, (((0,), (0,)), ((), ())), precision=HIGH,
         preferred_element_type=f32,
     ).reshape(256, NX, B)
+    share = after(share, *ring[1])
 
     def share_of(t):
         return lax.dynamic_slice_in_dim(share, t, 1, axis=1).reshape(256, B)
@@ -158,6 +154,7 @@
     for d in range(NY):
         got = both if d == 0 else lax.ppermute(both, "col", shift_perm(NY, d))
         full = lax.dynamic_update_slice(full, got[None], (lax.rem(y + NY - d, NY), 0, 0))
+    full = after(full, *ring[2])
     product = full[:, :256].reshape(1024, B)
     picked_rows = full[:, 256:].reshape(8, 32, B).transpose(0, 2, 1).reshape(1024, 32)
 

time: 122 us -> 106 us (0.87)
  waiting for transfers between devices: 34.6 us -> 20.8 us
    ppermute x3 -> x0, starting transfers between devices: 10.3 us -> none  [shards(): lax.ppermute(listed_for(lax.rem(y + d, NY)), ('z', 'col'), pairs)]
    all_to_all x1, waiting for transfers between devices: 7.16 us -> 0.01 us  [shards(): cut = lax.all_to_all(listed, ('z', 'x', 'col'), 0, 0, tiled=True)]
    ppermute x3, starting transfers between devices: 4.91 us -> 10.1 us  [shards(): down = lax.ppermute(down, 'z', shift_perm(NZ, -1))]
    ppermute x3, waiting for transfers between devices: 0.01 us -> 5.08 us  [shards(): got = pair if d == 0 else lax.ppermute(pair, 'col', shift_perm(NY, d))]
    ppermute x3, waiting for transfers between devices: 4.99 us -> 0.01 us  [shards(): up = lax.ppermute(up, 'z', shift_perm(NZ, 1))]
    ppermute x3, waiting for transfers between devices: 0.01 us -> 3.79 us  [shards(): lax.ppermute(child_rows, 'x', shift_perm(NX, d))]
    ppermute x3, waiting for transfers between devices: 5.66 us -> 2.08 us  [shards(): lax.ppermute(share_of(lax.rem(x + d, NX)), 'x', shift_perm(NX, d))]
    all_to_all x1, waiting for transfers between devices: 8.08 us -> 4.66 us  [shards(): wide = lax.all_to_all(wide, 'z', 0, 0, tiled=True)]
  transfers between devices with their start and end apart: 27 -> 24, of which waited for: 11 -> 9; matrix products, arithmetic and copies ran while one was open for 14% -> 13% of each run, Pallas kernels for 3% -> 4%
where the time goes in v3:
time: 106 us
  starting transfers between devices  58.6 us (55%)
  waiting for transfers between devices  20.8 us (20%)
  local copies, waits for them, and re-layouts  16.4 us (15%)
  matrix products  4.25 us (4%)
  Pallas kernels  3.72 us (4%)
    ppermute x3, starting transfers between devices, shards(): down = lax.ppermute(down, 'z', shift_perm(NZ, -1))  10.1 us
    dynamic_update_slice x9, local copies, waits for them, and re-layouts, place(): lax.dynamic_update_slice(whole, part[None], (lax.rem(z + 2 * NZ - d, NZ),...  9.51 us
    all_to_all x1, starting transfers between devices, shards(): cut = lax.all_to_all(listed, ('z', 'x', 'col'), 0, 0, tiled=True)  8.17 us
    all_to_all x1, starting transfers between devices, shards(): wide = lax.all_to_all(wide, 'z', 0, 0, tiled=True)  6.21 us
    ppermute x3, starting transfers between devices, shards(): lax.ppermute(child_rows, 'x', shift_perm(NX, d))  5.73 us
    ppermute x3, waiting for transfers between devices, shards(): got = both if d == 0 else lax.ppermute(both, 'col', shift_perm(NY, d))  5.18 us
    ppermute x3, waiting for transfers between devices, shards(): got = pair if d == 0 else lax.ppermute(pair, 'col', shift_perm(NY, d))  5.08 us
    ppermute x3, starting transfers between devices, shards(): got = pair if d == 0 else lax.ppermute(pair, 'col', shift_perm(NY, d))  4.78 us
  transfers between devices with their start and end apart: 24, of which 9 were waited for; matrix products, arithmetic and copies ran while one was open for 13% of the time, Pallas kernels for 4%

profile of v3, /device:TPU:8, one launch (start us, length us, event | category | flops | bytes accessed | tf_op | source)
XLA Modules:
  0.0 105.7 jit_solution(14375623121598847648)
XLA Ops:
  0.6 1.6 %collective-permute-start = (f32[32,1024]{1,0:T(8,128)}, f32[32,1024]{1,0:T(8,128)S(1)}, u32[]{:S(2)}, u32[]{:S(2)}) collective-permute-start(f32[32,1024]{1,0:T(8,128)} %param.6), channel_id=1, source_target_pairs={{0,4},{4,8},{8,12},{12,0},{1,5},{5,9},{9,13},{13,1},{2,6},{6,10},{... | collective-permute-start | bytes 393224 | tf_op jit(solution)/shard_map/ppermute | solution.py:56
  2.2 2.7 %collective-permute-start.1 = (f32[32,1024]{1,0:T(8,128)}, f32[32,1024]{1,0:T(8,128)S(1)}, u32[]{:S(2)}, u32[]{:S(2)}) collective-permute-start(f32[32,1024]{1,0:T(8,128)} %param.6), channel_id=1, source_target_pairs={{0,8},{4,12},{8,0},{12,4},{1,9},{5,13},{9,1},{13,5},{2,10},{6,14},... | collective-permute-start | bytes 393224 | tf_op jit(solution)/shard_map/ppermute | solution.py:56
  4.9 1.4 %collective-permute-start.2 = (f32[32,1024]{1,0:T(8,128)}, f32[32,1024]{1,0:T(8,128)S(1)}, u32[]{:S(2)}, u32[]{:S(2)}) collective-permute-start(f32[32,1024]{1,0:T(8,128)} %param.6), channel_id=1, source_target_pairs={{0,12},{4,0},{8,4},{12,8},{1,13},{5,1},{9,5},{13,9},{2,14},{6,2},{... | collective-permute-start | bytes 393224 | tf_op jit(solution)/shard_map/ppermute | solution.py:56
  7.5 3.6 %collective-permute-done.1 = f32[32,1024]{1,0:T(8,128)S(1)} collective-permute-done((f32[32,1024]{1,0:T(8,128)}, f32[32,1024]{1,0:T(8,128)S(1)}, u32[]{:S(2)}, u32[]{:S(2)}) %collective-permute-start.1) | collective-permute-done | bytes 131104 | tf_op jit(solution)/shard_map/ppermute | solution.py:56
  11.2 1.0 reshape.140
  12.4 4.6 %collective-permute-start.6 = (f32[32,512]{1,0:T(8,128)S(1)}, f32[32,512]{1,0:T(8,128)S(1)}, u32[]{:S(2)}, u32[]{:S(2)}) collective-permute-start(f32[32,512]{1,0:T(8,128)S(1)} %bitcast.117), channel_id=1, source_target_pairs={{0,16},{1,48},{2,80},{3,112},{4,20},{5,52},{6,84},{7,116},{8,24},{... | collective-permute-start | bytes 196616 | tf_op jit(solution)/shard_map/ppermute | solution.py:79
  17.0 3.3 %collective-permute-start.5 = (f32[32,512]{1,0:T(8,128)S(1)}, f32[32,512]{1,0:T(8,128)S(1)}, u32[]{:S(2)}, u32[]{:S(2)}) collective-permute-start(f32[32,512]{1,0:T(8,128)S(1)} %bitcast.118), channel_id=1, source_target_pairs={{0,0},{1,32},{2,64},{3,96},{4,4},{5,36},{6,68},{7,100},{8,8},{9,40... | collective-permute-start | bytes 196616 | tf_op jit(solution)/shard_map/ppermute | solution.py:75
  20.3 1.9 %shard_map.59 = f32[2,4,4,4,8,128]{5,4,3,2,1,0:T(8,128)} custom-call(s32[8]{0:T(128)} %pattern_ref.3, s32[1]{0:T(128)} %bitcast.1.y_ref, f32[128,1024]{1,0:T(8,128)} %root_ref.1), custom_call_target="tpu_custom_call" | custom-call | tf_op jit(solution)/shard_map/pallas_call | solution.py:114
  23.1 6.8 %collective-permute-start.4 = (f32[128,1024]{1,0:T(8,128)S(1)}, f32[128,1024]{1,0:T(8,128)S(1)}, u32[]{:S(2)}, u32[]{:S(2)}) collective-permute-start(f32[128,1024]{1,0:T(8,128)S(1)} %bitcast.103), channel_id=1, source_target_pairs={{0,112},{16,0},{32,16},{48,32},{64,48},{80,64},{96,80},{112,96},{1... | collective-permute-start | bytes 1572872 | tf_op jit(solution)/shard_map/ppermute | solution.py:104
  29.9 8.2 %all-to-all-start = ((f32[128,8,128]{2,1,0:T(8,128)}), f32[128,8,128]{2,1,0:T(8,128)S(1)}, u32[]{:S(2)}, u32[]{:S(2)}) async-start(f32[128,8,128]{2,1,0:T(8,128)} %bitcast.99), calls=%async_computation | async-start | bytes 1048576 | tf_op jit(solution)/shard_map/all_to_all | solution.py:121
  38.1 1.5 %collective-permute-start.7 = (f32[2,32,512]{2,1,0:T(8,128)S(1)}, f32[2,32,512]{2,1,0:T(8,128)S(1)}, u32[]{:S(2)}, u32[]{:S(2)}) collective-permute-start(f32[2,32,512]{2,1,0:T(8,128)S(1)} %maximum_select_fusion.1), channel_id=1, source_target_pairs={{0,1},{1,2},{2,3},{3,0},{4,5},{5,6},{6,7},{7,4},{8,9},{9,10},{10,1... | collective-permute-start | bytes 393224 | tf_op jit(solution)/shard_map/ppermute | solution.py:86
  39.6 2.5 %broadcast_in_dim.84 = f32[8,128,1024]{2,1,0:T(8,128)} broadcast(f32[]{:T(128)} %constant.103.clone.1), dimensions={} | broadcast | bytes 4194308 | tf_op jit(solution)/shard_map/broadcast_in_dim | solution.py:92
  43.0 1.5 %collective-permute-start.8 = (f32[2,32,512]{2,1,0:T(8,128)S(1)}, f32[2,32,512]{2,1,0:T(8,128)S(1)}, u32[]{:S(2)}, u32[]{:S(2)}) collective-permute-start(f32[2,32,512]{2,1,0:T(8,128)S(1)} %maximum_select_fusion.1), channel_id=1, source_target_pairs={{0,2},{1,3},{2,0},{3,1},{4,6},{5,7},{6,4},{7,5},{8,10},{9,11},{10,... | collective-permute-start | bytes 393224 | tf_op jit(solution)/shard_map/ppermute | solution.py:86
  44.5 1.7 %collective-permute-start.9 = (f32[2,32,512]{2,1,0:T(8,128)S(1)}, f32[2,32,512]{2,1,0:T(8,128)S(1)}, u32[]{:S(2)}, u32[]{:S(2)}) collective-permute-start(f32[2,32,512]{2,1,0:T(8,128)S(1)} %maximum_select_fusion.1), channel_id=1, source_target_pairs={{0,3},{1,0},{2,1},{3,2},{4,7},{5,4},{6,5},{7,6},{8,11},{9,8},{10,9... | collective-permute-start | bytes 393224 | tf_op jit(solution)/shard_map/ppermute | solution.py:86
  46.3 5.1 %collective-permute-done.8 = f32[2,32,512]{2,1,0:T(8,128)S(1)} collective-permute-done((f32[2,32,512]{2,1,0:T(8,128)S(1)}, f32[2,32,512]{2,1,0:T(8,128)S(1)}, u32[]{:S(2)}, u32[]{:S(2)}) %collective-permute-start.8) | collective-permute-done | bytes 131104 | tf_op jit(solution)/shard_map/ppermute | solution.py:86
  51.4 1.6 %collective-permute-start.10 = (f32[128,1024]{1,0:T(8,128)S(1)}, f32[128,1024]{1,0:T(8,128)}, u32[]{:S(2)}, u32[]{:S(2)}) collective-permute-start(f32[128,1024]{1,0:T(8,128)S(1)} %collective-permute-done.3), channel_id=1, source_target_pairs={{0,16},{16,32},{32,48},{48,64},{64,80},{80,96},{96,112},{112,0},{1... | collective-permute-start | bytes 1572872 | tf_op jit(solution)/shard_map/ppermute | solution.py:103
  53.0 1.9 %collective-permute-start.11 = (f32[128,1024]{1,0:T(8,128)S(1)}, f32[128,1024]{1,0:T(8,128)}, u32[]{:S(2)}, u32[]{:S(2)}) collective-permute-start(f32[128,1024]{1,0:T(8,128)S(1)} %collective-permute-done.4), channel_id=1, source_target_pairs={{0,112},{16,0},{32,16},{48,32},{64,48},{80,64},{96,80},{112,96},{1... | collective-permute-start | bytes 1572872 | tf_op jit(solution)/shard_map/ppermute | solution.py:104
  57.6 1.8 %shard_map.60 = f32[8,8,8,128]{3,2,1,0:T(8,128)} custom-call(s32[8]{0:T(128)} %pattern_ref.3, s32[1]{0:T(128)} %bitcast.m_ref, f32[128,8,128]{2,1,0:T(8,128)} %copy-done), custom_call_target="tpu_custom_call" | custom-call | tf_op jit(solution)/shard_map/pallas_call | solution.py:122
  59.4 6.2 %all-to-all-start.1 = ((f32[8,64,128]{2,1,0:T(8,128)}), f32[8,64,128]{2,1,0:T(8,128)S(1)}, u32[]{:S(2)}, u32[]{:S(2)}) async-start(f32[8,64,128]{2,1,0:T(8,128)} %bitcast.108), calls=%async_computation.1 | async-start | bytes 524288 | tf_op jit(solution)/shard_map/all_to_all | solution.py:129
  65.6 2.0 %collective-permute-start.18 = (f32[128,1024]{1,0:T(8,128)}, f32[128,1024]{1,0:T(8,128)S(1)}, u32[]{:S(2)}, u32[]{:S(2)}) collective-permute-start(f32[128,1024]{1,0:T(8,128)} %collective-permute-done.10), channel_id=1, source_target_pairs={{0,16},{16,32},{32,48},{48,64},{64,80},{80,96},{96,112},{112,0},{1... | collective-permute-start | bytes 1572872 | tf_op jit(solution)/shard_map/ppermute | solution.py:103
  67.6 1.5 %collective-permute-start.19 = (f32[128,1024]{1,0:T(8,128)}, f32[128,1024]{1,0:T(8,128)S(1)}, u32[]{:S(2)}, u32[]{:S(2)}) collective-permute-start(f32[128,1024]{1,0:T(8,128)} %collective-permute-done.11), channel_id=1, source_target_pairs={{0,112},{16,0},{32,16},{48,32},{64,48},{80,64},{96,80},{112,96},{1... | collective-permute-start | bytes 1572872 | tf_op jit(solution)/shard_map/ppermute | solution.py:104
  69.1 1.9 %bitcast_dynamic-update-slice_fusion.3 = f32[8,128,1024]{2,1,0:T(8,128)} fusion(f32[8,128,1024]{2,1,0:T(8,128)} %bitcast_dynamic-update-slice_fusion.4, s32[]{:T(128)S(6)} %select_n.112, f32[128,1024]{1,0:T(8,128)} %collective-permute-done.10), kind=kLoop, calls=%fused_computation.8 | loop fusion | bytes 1048580 | tf_op jit(solution)/shard_map/dynamic_update_slice | solution.py:95
  71.0 1.9 %bitcast_dynamic-update-slice_fusion.2 = f32[8,128,1024]{2,1,0:T(8,128)} fusion(f32[8,128,1024]{2,1,0:T(8,128)} %bitcast_dynamic-update-slice_fusion.3, s32[]{:T(128)S(6)} %select_n.113, f32[128,1024]{1,0:T(8,128)} %collective-permute-done.11), kind=kLoop, calls=%fused_computation.7 | loop fusion | bytes 1048580 | tf_op jit(solution)/shard_map/dynamic_update_slice | solution.py:95
  72.9 4.7 %all-to-all-done.1 = f32[8,64,128]{2,1,0:T(8,128)S(1)} async-done(((f32[8,64,128]{2,1,0:T(8,128)}), f32[8,64,128]{2,1,0:T(8,128)S(1)}, u32[]{:S(2)}, u32[]{:S(2)}) %all-to-all-start.1) | async-done | bytes 262176 | tf_op jit(solution)/shard_map/all_to_all | solution.py:129
  78.4 2.4 %collective-permute-start.14 = (f32[256,128]{1,0:T(8,128)S(1)}, f32[256,128]{1,0:T(8,128)S(1)}, u32[]{:S(2)}, u32[]{:S(2)}) collective-permute-start(f32[256,128]{1,0:T(8,128)S(1)} %get-tuple-element.13), channel_id=1, source_target_pairs={{0,12},{4,0},{8,4},{12,8},{1,13},{5,1},{9,5},{13,9},{2,14},{6,2},{... | collective-permute-start | bytes 393224 | tf_op jit(solution)/shard_map/ppermute | solution.py:146
  80.8 1.0 collective-permute-start.13
  83.0 2.7 %collective-permute-start.21 = (f32[128,512]{1,0:T(8,128)S(1)}, f32[128,512]{1,0:T(8,128)S(1)}, u32[]{:S(2)}, u32[]{:S(2)}) collective-permute-start(f32[128,512]{1,0:T(8,128)S(1)} %slice.25), channel_id=1, source_target_pairs={{0,112},{16,0},{32,16},{48,32},{64,48},{80,64},{96,80},{112,96},{1... | collective-permute-start | bytes 786440 | tf_op jit(solution)/shard_map/ppermute | solution.py:109
  87.3 1.3 %collective-permute-done.12 = f32[256,128]{1,0:T(8,128)S(1)} collective-permute-done((f32[256,128]{1,0:T(8,128)S(1)}, f32[256,128]{1,0:T(8,128)S(1)}, u32[]{:S(2)}, u32[]{:S(2)}) %collective-permute-start.12) | collective-permute-done | bytes 131104 | tf_op jit(solution)/shard_map/ppermute | solution.py:146
  90.2 2.3 %collective-permute-start.16 = (f32[320,128]{1,0:T(8,128)S(1)}, f32[320,128]{1,0:T(8,128)S(1)}, u32[]{:S(2)}, u32[]{:S(2)}) collective-permute-start(f32[320,128]{1,0:T(8,128)S(1)} %pad_maximum_fusion), channel_id=1, source_target_pairs={{0,2},{1,3},{2,0},{3,1},{4,6},{5,7},{6,4},{7,5},{8,10},{9,11},{10,... | collective-permute-start | bytes 491528 | tf_op jit(solution)/shard_map/ppermute | solution.py:155
  94.1 3.0 %collective-permute-done.16 = f32[320,128]{1,0:T(8,128)S(1)} collective-permute-done((f32[320,128]{1,0:T(8,128)S(1)}, f32[320,128]{1,0:T(8,128)S(1)}, u32[]{:S(2)}, u32[]{:S(2)}) %collective-permute-start.16) | collective-permute-done | bytes 163872 | tf_op jit(solution)/shard_map/ppermute | solution.py:155
  97.1 1.6 %collective-permute-done.17 = f32[320,128]{1,0:T(8,128)S(1)} collective-permute-done((f32[320,128]{1,0:T(8,128)S(1)}, f32[320,128]{1,0:T(8,128)S(1)}, u32[]{:S(2)}, u32[]{:S(2)}) %collective-permute-start.17) | collective-permute-done | bytes 163872 | tf_op jit(solution)/shard_map/ppermute | solution.py:155
  100.6 3.6 %fusion = f32[160,1024]{1,0:T(8,128)S(1)} fusion(f32[1024,1024]{1,0:T(8,128)} %bitcast.53, f32[1024,32]{1,0:T(8,128)S(1)} %bitcast.97, f32[1024,128]{1,0:T(8,128)S(1)} %bitcast.98), kind=kOutput, calls=%fused_computation | convolution fusion | flops 1006796800 | bytes 5505024 | tf_op jit(solution)/shard_map/dot_general | solution.py:161
  (69 shorter events, 15.9 us)
Async XLA Ops:
  0.6 6.9 %collective-permute-start = (f32[32,1024]{1,0:T(8,128)}, f32[32,1024]{1,0:T(8,128)S(1)}, u32[]{:S(2)}, u32[]{:S(2)}) collective-permute-start(f32[32,1024]{1,0:T(8,128)} %param.6), channel_id=1, source_target_pairs={{0,4},{4,8},{8,12},{12,0},{1,5},{5,9},{9,13},{13,1},{2,6},{6,10},{... | collective-permute-start | bytes 393224 | tf_op jit(solution)/shard_map/ppermute | solution.py:56
  2.2 9.0 %collective-permute-start.1 = (f32[32,1024]{1,0:T(8,128)}, f32[32,1024]{1,0:T(8,128)S(1)}, u32[]{:S(2)}, u32[]{:S(2)}) collective-permute-start(f32[32,1024]{1,0:T(8,128)} %param.6), channel_id=1, source_target_pairs={{0,8},{4,12},{8,0},{12,4},{1,9},{5,13},{9,1},{13,5},{2,10},{6,14},... | collective-permute-start | bytes 393224 | tf_op jit(solution)/shard_map/ppermute | solution.py:56
  4.9 6.2 %collective-permute-start.2 = (f32[32,1024]{1,0:T(8,128)}, f32[32,1024]{1,0:T(8,128)S(1)}, u32[]{:S(2)}, u32[]{:S(2)}) collective-permute-start(f32[32,1024]{1,0:T(8,128)} %param.6), channel_id=1, source_target_pairs={{0,12},{4,0},{8,4},{12,8},{1,13},{5,1},{9,5},{13,9},{2,14},{6,2},{... | collective-permute-start | bytes 393224 | tf_op jit(solution)/shard_map/ppermute | solution.py:56
  12.4 25.7 %collective-permute-start.6 = (f32[32,512]{1,0:T(8,128)S(1)}, f32[32,512]{1,0:T(8,128)S(1)}, u32[]{:S(2)}, u32[]{:S(2)}) collective-permute-start(f32[32,512]{1,0:T(8,128)S(1)} %bitcast.117), channel_id=1, source_target_pairs={{0,16},{1,48},{2,80},{3,112},{4,20},{5,52},{6,84},{7,116},{8,24},{... | collective-permute-start | bytes 196616 | tf_op jit(solution)/shard_map/ppermute | solution.py:79
  17.0 21.1 %collective-permute-start.5 = (f32[32,512]{1,0:T(8,128)S(1)}, f32[32,512]{1,0:T(8,128)S(1)}, u32[]{:S(2)}, u32[]{:S(2)}) collective-permute-start(f32[32,512]{1,0:T(8,128)S(1)} %bitcast.118), channel_id=1, source_target_pairs={{0,0},{1,32},{2,64},{3,96},{4,4},{5,36},{6,68},{7,100},{8,8},{9,40... | collective-permute-start | bytes 196616 | tf_op jit(solution)/shard_map/ppermute | solution.py:75
  22.3 29.2 %collective-permute-start.3 = (f32[128,1024]{1,0:T(8,128)S(1)}, f32[128,1024]{1,0:T(8,128)S(1)}, u32[]{:S(2)}, u32[]{:S(2)}) collective-permute-start(f32[128,1024]{1,0:T(8,128)S(1)} %bitcast.102), channel_id=1, source_target_pairs={{0,16},{16,32},{32,48},{48,64},{64,80},{80,96},{96,112},{112,0},{1... | collective-permute-start | bytes 1572872 | tf_op jit(solution)/shard_map/ppermute | solution.py:103
  23.1 29.9 %collective-permute-start.4 = (f32[128,1024]{1,0:T(8,128)S(1)}, f32[128,1024]{1,0:T(8,128)S(1)}, u32[]{:S(2)}, u32[]{:S(2)}) collective-permute-start(f32[128,1024]{1,0:T(8,128)S(1)} %bitcast.103), channel_id=1, source_target_pairs={{0,112},{16,0},{32,16},{48,32},{64,48},{80,64},{96,80},{112,96},{1... | collective-permute-start | bytes 1572872 | tf_op jit(solution)/shard_map/ppermute | solution.py:104
  29.9 26.9 %all-to-all-start = ((f32[128,8,128]{2,1,0:T(8,128)}), f32[128,8,128]{2,1,0:T(8,128)S(1)}, u32[]{:S(2)}, u32[]{:S(2)}) async-start(f32[128,8,128]{2,1,0:T(8,128)} %bitcast.99), calls=%async_computation | async-start | bytes 1048576 | tf_op jit(solution)/shard_map/all_to_all | solution.py:121
  38.1 8.2 %collective-permute-start.7 = (f32[2,32,512]{2,1,0:T(8,128)S(1)}, f32[2,32,512]{2,1,0:T(8,128)S(1)}, u32[]{:S(2)}, u32[]{:S(2)}) collective-permute-start(f32[2,32,512]{2,1,0:T(8,128)S(1)} %maximum_select_fusion.1), channel_id=1, source_target_pairs={{0,1},{1,2},{2,3},{3,0},{4,5},{5,6},{6,7},{7,4},{8,9},{9,10},{10,1... | collective-permute-start | bytes 393224 | tf_op jit(solution)/shard_map/ppermute | solution.py:86
  43.0 8.4 %collective-permute-start.8 = (f32[2,32,512]{2,1,0:T(8,128)S(1)}, f32[2,32,512]{2,1,0:T(8,128)S(1)}, u32[]{:S(2)}, u32[]{:S(2)}) collective-permute-start(f32[2,32,512]{2,1,0:T(8,128)S(1)} %maximum_select_fusion.1), channel_id=1, source_target_pairs={{0,2},{1,3},{2,0},{3,1},{4,6},{5,7},{6,4},{7,5},{8,10},{9,11},{10,... | collective-permute-start | bytes 393224 | tf_op jit(solution)/shard_map/ppermute | solution.py:86
  44.5 10.4 %collective-permute-start.9 = (f32[2,32,512]{2,1,0:T(8,128)S(1)}, f32[2,32,512]{2,1,0:T(8,128)S(1)}, u32[]{:S(2)}, u32[]{:S(2)}) collective-permute-start(f32[2,32,512]{2,1,0:T(8,128)S(1)} %maximum_select_fusion.1), channel_id=1, source_target_pairs={{0,3},{1,0},{2,1},{3,2},{4,7},{5,4},{6,5},{7,6},{8,11},{9,8},{10,9... | collective-permute-start | bytes 393224 | tf_op jit(solution)/shard_map/ppermute | solution.py:86
  51.4 14.2 %collective-permute-start.10 = (f32[128,1024]{1,0:T(8,128)S(1)}, f32[128,1024]{1,0:T(8,128)}, u32[]{:S(2)}, u32[]{:S(2)}) collective-permute-start(f32[128,1024]{1,0:T(8,128)S(1)} %collective-permute-done.3), channel_id=1, source_target_pairs={{0,16},{16,32},{32,48},{48,64},{64,80},{80,96},{96,112},{112,0},{1... | collective-permute-start | bytes 1572872 | tf_op jit(solution)/shard_map/ppermute | solution.py:103
  53.0 14.6 %collective-permute-start.11 = (f32[128,1024]{1,0:T(8,128)S(1)}, f32[128,1024]{1,0:T(8,128)}, u32[]{:S(2)}, u32[]{:S(2)}) collective-permute-start(f32[128,1024]{1,0:T(8,128)S(1)} %collective-permute-done.4), channel_id=1, source_target_pairs={{0,112},{16,0},{32,16},{48,32},{64,48},{80,64},{96,80},{112,96},{1... | collective-permute-start | bytes 1572872 | tf_op jit(solution)/shard_map/ppermute | solution.py:104
  56.8 0.8 copy-start
  59.4 18.2 %all-to-all-start.1 = ((f32[8,64,128]{2,1,0:T(8,128)}), f32[8,64,128]{2,1,0:T(8,128)S(1)}, u32[]{:S(2)}, u32[]{:S(2)}) async-start(f32[8,64,128]{2,1,0:T(8,128)} %bitcast.108), calls=%async_computation.1 | async-start | bytes 524288 | tf_op jit(solution)/shard_map/all_to_all | solution.py:129
  65.6 16.7 %collective-permute-start.18 = (f32[128,1024]{1,0:T(8,128)}, f32[128,1024]{1,0:T(8,128)S(1)}, u32[]{:S(2)}, u32[]{:S(2)}) collective-permute-start(f32[128,1024]{1,0:T(8,128)} %collective-permute-done.10), channel_id=1, source_target_pairs={{0,16},{16,32},{32,48},{48,64},{64,80},{80,96},{96,112},{112,0},{1... | collective-permute-start | bytes 1572872 | tf_op jit(solution)/shard_map/ppermute | solution.py:103
  67.6 15.3 %collective-permute-start.19 = (f32[128,1024]{1,0:T(8,128)}, f32[128,1024]{1,0:T(8,128)S(1)}, u32[]{:S(2)}, u32[]{:S(2)}) collective-permute-start(f32[128,1024]{1,0:T(8,128)} %collective-permute-done.11), channel_id=1, source_target_pairs={{0,112},{16,0},{32,16},{48,32},{64,48},{80,64},{96,80},{112,96},{1... | collective-permute-start | bytes 1572872 | tf_op jit(solution)/shard_map/ppermute | solution.py:104
  78.4 8.2 %collective-permute-start.14 = (f32[256,128]{1,0:T(8,128)S(1)}, f32[256,128]{1,0:T(8,128)S(1)}, u32[]{:S(2)}, u32[]{:S(2)}) collective-permute-start(f32[256,128]{1,0:T(8,128)S(1)} %get-tuple-element.13), channel_id=1, source_target_pairs={{0,12},{4,0},{8,4},{12,8},{1,13},{5,1},{9,5},{13,9},{2,14},{6,2},{... | collective-permute-start | bytes 393224 | tf_op jit(solution)/shard_map/ppermute | solution.py:146
  80.8 6.5 %collective-permute-start.13 = (f32[256,128]{1,0:T(8,128)S(1)}, f32[256,128]{1,0:T(8,128)S(1)}, u32[]{:S(2)}, u32[]{:S(2)}) collective-permute-start(f32[256,128]{1,0:T(8,128)S(1)} %get-tuple-element.14), channel_id=1, source_target_pairs={{0,8},{4,12},{8,0},{12,4},{1,9},{5,13},{9,1},{13,5},{2,10},{6,14},... | collective-permute-start | bytes 393224 | tf_op jit(solution)/shard_map/ppermute | solution.py:146
  81.7 6.9 %collective-permute-start.12 = (f32[256,128]{1,0:T(8,128)S(1)}, f32[256,128]{1,0:T(8,128)S(1)}, u32[]{:S(2)}, u32[]{:S(2)}) collective-permute-start(f32[256,128]{1,0:T(8,128)S(1)} %get-tuple-element.12), channel_id=1, source_target_pairs={{0,4},{4,8},{8,12},{12,0},{1,5},{5,9},{9,13},{13,1},{2,6},{6,10},{... | collective-permute-start | bytes 393224 | tf_op jit(solution)/shard_map/ppermute | solution.py:146
  82.3 16.7 %collective-permute-start.20 = (f32[128,512]{1,0:T(8,128)S(1)}, f32[128,512]{1,0:T(8,128)S(1)}, u32[]{:S(2)}, u32[]{:S(2)}) collective-permute-start(f32[128,512]{1,0:T(8,128)S(1)} %slice.24), channel_id=1, source_target_pairs={{0,16},{16,32},{32,48},{48,64},{64,80},{80,96},{96,112},{112,0},{1... | collective-permute-start | bytes 786440 | tf_op jit(solution)/shard_map/ppermute | solution.py:108
  83.0 16.8 %collective-permute-start.21 = (f32[128,512]{1,0:T(8,128)S(1)}, f32[128,512]{1,0:T(8,128)S(1)}, u32[]{:S(2)}, u32[]{:S(2)}) collective-permute-start(f32[128,512]{1,0:T(8,128)S(1)} %slice.25), channel_id=1, source_target_pairs={{0,112},{16,0},{32,16},{48,32},{64,48},{80,64},{96,80},{112,96},{1... | collective-permute-start | bytes 786440 | tf_op jit(solution)/shard_map/ppermute | solution.py:109
  88.7 5.4 %collective-permute-start.15 = (f32[320,128]{1,0:T(8,128)S(1)}, f32[320,128]{1,0:T(8,128)S(1)}, u32[]{:S(2)}, u32[]{:S(2)}) collective-permute-start(f32[320,128]{1,0:T(8,128)S(1)} %pad_maximum_fusion), channel_id=1, source_target_pairs={{0,1},{1,2},{2,3},{3,0},{4,5},{5,6},{6,7},{7,4},{8,9},{9,10},{10,1... | collective-permute-start | bytes 491528 | tf_op jit(solution)/shard_map/ppermute | solution.py:155
  90.2 6.9 %collective-permute-start.16 = (f32[320,128]{1,0:T(8,128)S(1)}, f32[320,128]{1,0:T(8,128)S(1)}, u32[]{:S(2)}, u32[]{:S(2)}) collective-permute-start(f32[320,128]{1,0:T(8,128)S(1)} %pad_maximum_fusion), channel_id=1, source_target_pairs={{0,2},{1,3},{2,0},{3,1},{4,6},{5,7},{6,4},{7,5},{8,10},{9,11},{10,... | collective-permute-start | bytes 491528 | tf_op jit(solution)/shard_map/ppermute | solution.py:155
  92.5 6.2 %collective-permute-start.17 = (f32[320,128]{1,0:T(8,128)S(1)}, f32[320,128]{1,0:T(8,128)S(1)}, u32[]{:S(2)}, u32[]{:S(2)}) collective-permute-start(f32[320,128]{1,0:T(8,128)S(1)} %pad_maximum_fusion), channel_id=1, source_target_pairs={{0,3},{1,0},{2,1},{3,2},{4,7},{5,4},{6,5},{7,6},{8,11},{9,8},{10,9... | collective-permute-start | bytes 491528 | tf_op jit(solution)/shard_map/ppermute | solution.py:155
  98.8 6.0 %copy-start.1 = (f32[128,1024]{1,0:T(8,128)S(1)}, f32[128,1024]{1,0:T(8,128)}, u32[]{:S(2)}) copy-start(f32[128,1024]{1,0:T(8,128)} %param.7) | copy-start | bytes 1572868

commit v4 on v3

--- a/solution.py
+++ b/solution.py
@@ -36,6 +36,32 @@
     for t in range(NZ):
         for j in range(8):
             out_ref[t, j] = rows[j]
+
+
+def last_kernel(
+    far_ref, product_ref, rows_ref, block_ref, left_ref, right_ref, inverse_ref,
+    coupling_ref, out_ref, hi, lo,
+):
+    @pl.when(pl.program_id(0) == 0)
+    def _():
+        left = jnp.concatenate([product_ref[...].T, -rows_ref[...]], axis=0)
+        high = left.astype(jnp.bfloat16)
+        hi[...] = high
+        lo[...] = (left - high.astype(jnp.float32)).astype(jnp.bfloat16)
+
+    def dot(a, b):
+        return jnp.dot(a, b, preferred_element_type=jnp.float32)
+
+    def dot3(a_high, a_low, block):
+        high = block.astype(jnp.bfloat16)
+        low = (block - high.astype(jnp.float32)).astype(jnp.bfloat16)
+        return dot(a_high, low) + dot(a_low, high) + dot(a_high, high)
+
+    far = pl.ds(pl.multiple_of(far_ref[0] * B, B), B)
+    half = jnp.where(pl.program_id(0) < 2, left_ref[...], right_ref[...])
+    total = dot3(hi[...], lo[...], block_ref[...]) + dot3(hi[:, far], lo[:, far], half)
+    out_ref[...] = inverse_ref[...] + total[:B]
+    coupling_ref[...] = total[B:]
 
 
 def scalar_spec():
@@ -64,7 +90,8 @@
 
     e = lax.rem(z, 2)
     high = z // 4
-    halves = after(child_rows, block).reshape(32, 2, 512)
+    turned = after(child_rows, block)
+    first, second = turned[:, :512], turned[:, 512:]
     places = [(a, b, c) for a in range(NZ) for b in range(NX) for c in range(NY)]
     straight = [
         (zxy(a, b, c), zxy(2 * c + a // 4, b, a % 4)) for a, b, c in places
@@ -73,11 +100,11 @@
         (zxy(a, b, c), zxy(2 * c + 1 - a // 4, b, a % 4)) for a, b, c in places
     ]
     mine = lax.ppermute(
-        lax.dynamic_slice_in_dim(halves, high, 1, axis=1).reshape(32, 512),
+        jnp.where(high == 0, first, second),
         ("z", "x", "col"), straight,
     )
     other = lax.ppermute(
-        lax.dynamic_slice_in_dim(halves, 1 - high, 1, axis=1).reshape(32, 512),
+        jnp.where(high == 0, second, first),
         ("z", "x", "col"), crossed,
     )
     pair = jnp.where(e == 0, jnp.stack([mine, other]), jnp.stack([other, mine]))
@@ -107,8 +134,6 @@
         gathered = place(gathered, down, -step)
     left = lax.ppermute(up[:, :512], "z", shift_perm(NZ, 1))
     right = lax.ppermute(down[:, 512:], "z", shift_perm(NZ, -1))
-    gathered = place(gathered, left, 4)
-    gathered = place(gathered, right, 4, 512)
     gathered = gathered.reshape(1024, 1024)
 
     listed = pl.pallas_call(
@@ -154,15 +179,35 @@
     for d in range(NY):
         got = both if d == 0 else lax.ppermute(both, "col", shift_perm(NY, d))
         full = lax.dynamic_update_slice(full, got[None], (lax.rem(y + NY - d, NY), 0, 0))
-    full = after(full, *ring[2])
+    full = after(full, gathered)
     product = full[:, :256].reshape(1024, B)
-    picked_rows = full[:, 256:].reshape(8, 32, B).transpose(0, 2, 1).reshape(1024, 32)
-
-    last = lax.dot_general(
-        jnp.concatenate([product, -picked_rows], axis=1), gathered,
-        (((0,), (0,)), ((), ())), precision=HIGH, preferred_element_type=f32,
-    )
-    return last[B:], child_inverse + last[:B]
+    picked_rows = full[:, 256:].reshape(8, 32, B).transpose(1, 0, 2).reshape(32, 1024)
+
+    opposite = lax.rem(z + 4, NZ).astype(jnp.int32).reshape(1)
+
+    def columns(height):
+        return pl.BlockSpec((height, 256), lambda i: (0, i))
+
+    return pl.pallas_call(
+        last_kernel,
+        grid=(4,),
+        out_shape=[
+            jax.ShapeDtypeStruct((32, 1024), f32),
+            jax.ShapeDtypeStruct((B, 1024), f32),
+        ],
+        in_specs=[
+            scalar_spec(),
+            pl.BlockSpec((1024, B), lambda i: (0, 0)),
+            pl.BlockSpec((32, 1024), lambda i: (0, 0)),
+            columns(1024),
+            pl.BlockSpec((B, 256), lambda i: (0, jnp.minimum(i, 1))),
+            pl.BlockSpec((B, 256), lambda i: (0, jnp.maximum(i - 2, 0))),
+            columns(B),
+        ],
+        out_specs=[columns(32), columns(B)],
+        scratch_shapes=[pltpu.VMEM((B + 32, 1024), jnp.bfloat16)] * 2,
+        compiler_params=pltpu.CompilerParams(vmem_limit_bytes=32 * 1024 * 1024),
+    )(opposite, product, picked_rows, gathered, left, right, child_inverse)
 
 
 def solution(mesh):

time: 106 us -> 104 us (0.981)
  Pallas kernels: 3.72 us -> 8.79 us
  local copies, waits for them, and re-layouts: 16.4 us -> 11.8 us
  matrix products: 4.25 us -> 0.64 us
  waiting for transfers between devices: 20.8 us -> 21.9 us
    pallas_call x0 -> x1, Pallas kernels: none -> 5.08 us  [shards(): pl.pallas_call(last_kernel, grid=(4,), out_shape=[jax.ShapeDtypeStruct((3...]
    dot_general x1 -> x0, matrix products: 3.61 us -> none  [shards(): lax.dot_general(jnp.concatenate([product, -picked_rows], axis=1), gathere...]
    dynamic_update_slice x9 -> x7, local copies, waits for them, and re-layouts: 9.51 us -> 6.93 us  [place(): lax.dynamic_update_slice(whole, part[None], (lax.rem(z + 2 * NZ - d, NZ),...]
  transfers between devices with their start and end apart: 24 -> 24, of which waited for: 9 -> 9; matrix products, arithmetic and copies ran while one was open for 13% -> 11% of each run, Pallas kernels for 4% -> 4%
where the time goes in v4:
time: 104 us
  starting transfers between devices  58.6 us (56%)
  waiting for transfers between devices  21.9 us (21%)
  local copies, waits for them, and re-layouts  11.8 us (11%)
  Pallas kernels  8.79 us (8%)
    ppermute x3, starting transfers between devices, shards(): down = lax.ppermute(down, 'z', shift_perm(NZ, -1))  10.1 us
    all_to_all x1, starting transfers between devices, shards(): cut = lax.all_to_all(listed, ('z', 'x', 'col'), 0, 0, tiled=True)  8.16 us
    dynamic_update_slice x7, local copies, waits for them, and re-layouts, place(): lax.dynamic_update_slice(whole, part[None], (lax.rem(z + 2 * NZ - d, NZ),...  6.93 us
    all_to_all x1, starting transfers between devices, shards(): wide = lax.all_to_all(wide, 'z', 0, 0, tiled=True)  6.22 us
    ppermute x3, starting transfers between devices, shards(): lax.ppermute(child_rows, 'x', shift_perm(NX, d))  5.73 us
    all_to_all x1, waiting for transfers between devices, shards(): wide = lax.all_to_all(wide, 'z', 0, 0, tiled=True)  5.71 us
    ppermute x3, waiting for transfers between devices, shards(): got = both if d == 0 else lax.ppermute(both, 'col', shift_perm(NY, d))  5.18 us
    ppermute x3, waiting for transfers between devices, shards(): got = pair if d == 0 else lax.ppermute(pair, 'col', shift_perm(NY, d))  5.08 us
  transfers between devices with their start and end apart: 24, of which 9 were waited for; matrix products, arithmetic and copies ran while one was open for 11% of the time, Pallas kernels for 4%

profile of v4, /device:TPU:8, one launch (start us, length us, event | category | flops | bytes accessed | tf_op | source)
XLA Modules:
  0.0 103.7 jit_solution(11977184290833763131)
XLA Ops:
  0.6 1.6 %collective-permute-start = (f32[32,1024]{1,0:T(8,128)}, f32[32,1024]{1,0:T(8,128)S(1)}, u32[]{:S(2)}, u32[]{:S(2)}) collective-permute-start(f32[32,1024]{1,0:T(8,128)} %param.6), channel_id=1, source_target_pairs={{0,4},{4,8},{8,12},{12,0},{1,5},{5,9},{9,13},{13,1},{2,6},{6,10},{... | collective-permute-start | bytes 393224 | tf_op jit(solution)/shard_map/ppermute | solution.py:82
  2.2 2.7 %collective-permute-start.1 = (f32[32,1024]{1,0:T(8,128)}, f32[32,1024]{1,0:T(8,128)S(1)}, u32[]{:S(2)}, u32[]{:S(2)}) collective-permute-start(f32[32,1024]{1,0:T(8,128)} %param.6), channel_id=1, source_target_pairs={{0,8},{4,12},{8,0},{12,4},{1,9},{5,13},{9,1},{13,5},{2,10},{6,14},... | collective-permute-start | bytes 393224 | tf_op jit(solution)/shard_map/ppermute | solution.py:82
  4.9 1.4 %collective-permute-start.2 = (f32[32,1024]{1,0:T(8,128)}, f32[32,1024]{1,0:T(8,128)S(1)}, u32[]{:S(2)}, u32[]{:S(2)}) collective-permute-start(f32[32,1024]{1,0:T(8,128)} %param.6), channel_id=1, source_target_pairs={{0,12},{4,0},{8,4},{12,8},{1,13},{5,1},{9,5},{13,9},{2,14},{6,2},{... | collective-permute-start | bytes 393224 | tf_op jit(solution)/shard_map/ppermute | solution.py:82
  6.4 0.9 bitcast_dynamic-update-slice_fusion.17
  7.5 3.6 %collective-permute-done.1 = f32[32,1024]{1,0:T(8,128)S(1)} collective-permute-done((f32[32,1024]{1,0:T(8,128)}, f32[32,1024]{1,0:T(8,128)S(1)}, u32[]{:S(2)}, u32[]{:S(2)}) %collective-permute-start.1) | collective-permute-done | bytes 131104 | tf_op jit(solution)/shard_map/ppermute | solution.py:82
  12.1 4.6 %collective-permute-start.6 = (f32[32,512]{1,0:T(8,128)S(1)}, f32[32,512]{1,0:T(8,128)S(1)}, u32[]{:S(2)}, u32[]{:S(2)}) collective-permute-start(f32[32,512]{1,0:T(8,128)S(1)} %get-tuple-element.16), channel_id=1, source_target_pairs={{0,16},{1,48},{2,80},{3,112},{4,20},{5,52},{6,84},{7,116},{8,24},{... | collective-permute-start | bytes 196616 | tf_op jit(solution)/shard_map/ppermute | solution.py:106
  16.7 3.3 %collective-permute-start.5 = (f32[32,512]{1,0:T(8,128)S(1)}, f32[32,512]{1,0:T(8,128)S(1)}, u32[]{:S(2)}, u32[]{:S(2)}) collective-permute-start(f32[32,512]{1,0:T(8,128)S(1)} %get-tuple-element.15), channel_id=1, source_target_pairs={{0,0},{1,32},{2,64},{3,96},{4,4},{5,36},{6,68},{7,100},{8,8},{9,40... | collective-permute-start | bytes 196616 | tf_op jit(solution)/shard_map/ppermute | solution.py:102
  20.0 1.9 %shard_map.59 = f32[2,4,4,4,8,128]{5,4,3,2,1,0:T(8,128)} custom-call(s32[8]{0:T(128)} %pattern_ref.3, s32[1]{0:T(128)} %bitcast.2.y_ref, f32[128,1024]{1,0:T(8,128)} %root_ref.1), custom_call_target="tpu_custom_call" | custom-call | tf_op jit(solution)/shard_map/pallas_call | solution.py:139
  22.9 6.8 %collective-permute-start.4 = (f32[128,1024]{1,0:T(8,128)S(1)}, f32[128,1024]{1,0:T(8,128)S(1)}, u32[]{:S(2)}, u32[]{:S(2)}) collective-permute-start(f32[128,1024]{1,0:T(8,128)S(1)} %bitcast.94), channel_id=1, source_target_pairs={{0,112},{16,0},{32,16},{48,32},{64,48},{80,64},{96,80},{112,96},{1... | collective-permute-start | bytes 1572872 | tf_op jit(solution)/shard_map/ppermute | solution.py:131
  29.6 8.2 %all-to-all-start = ((f32[128,8,128]{2,1,0:T(8,128)}), f32[128,8,128]{2,1,0:T(8,128)S(1)}, u32[]{:S(2)}, u32[]{:S(2)}) async-start(f32[128,8,128]{2,1,0:T(8,128)} %bitcast.90), calls=%async_computation | async-start | bytes 1048576 | tf_op jit(solution)/shard_map/all_to_all | solution.py:146
  37.8 1.5 %collective-permute-start.7 = (f32[2,32,512]{2,1,0:T(8,128)S(1)}, f32[2,32,512]{2,1,0:T(8,128)S(1)}, u32[]{:S(2)}, u32[]{:S(2)}) collective-permute-start(f32[2,32,512]{2,1,0:T(8,128)S(1)} %maximum_select_fusion.1), channel_id=1, source_target_pairs={{0,1},{1,2},{2,3},{3,0},{4,5},{5,6},{6,7},{7,4},{8,9},{9,10},{10,1... | collective-permute-start | bytes 393224 | tf_op jit(solution)/shard_map/ppermute | solution.py:113
  39.4 2.5 %broadcast_in_dim.78 = f32[8,128,1024]{2,1,0:T(8,128)} broadcast(f32[]{:T(128)} %constant.104.clone.1), dimensions={} | broadcast | bytes 4194308 | tf_op jit(solution)/shard_map/broadcast_in_dim | solution.py:119
  42.7 1.5 %collective-permute-start.8 = (f32[2,32,512]{2,1,0:T(8,128)S(1)}, f32[2,32,512]{2,1,0:T(8,128)S(1)}, u32[]{:S(2)}, u32[]{:S(2)}) collective-permute-start(f32[2,32,512]{2,1,0:T(8,128)S(1)} %maximum_select_fusion.1), channel_id=1, source_target_pairs={{0,2},{1,3},{2,0},{3,1},{4,6},{5,7},{6,4},{7,5},{8,10},{9,11},{10,... | collective-permute-start | bytes 393224 | tf_op jit(solution)/shard_map/ppermute | solution.py:113
  44.2 1.7 %collective-permute-start.9 = (f32[2,32,512]{2,1,0:T(8,128)S(1)}, f32[2,32,512]{2,1,0:T(8,128)S(1)}, u32[]{:S(2)}, u32[]{:S(2)}) collective-permute-start(f32[2,32,512]{2,1,0:T(8,128)S(1)} %maximum_select_fusion.1), channel_id=1, source_target_pairs={{0,3},{1,0},{2,1},{3,2},{4,7},{5,4},{6,5},{7,6},{8,11},{9,8},{10,9... | collective-permute-start | bytes 393224 | tf_op jit(solution)/shard_map/ppermute | solution.py:113
  46.1 5.1 %collective-permute-done.8 = f32[2,32,512]{2,1,0:T(8,128)S(1)} collective-permute-done((f32[2,32,512]{2,1,0:T(8,128)S(1)}, f32[2,32,512]{2,1,0:T(8,128)S(1)}, u32[]{:S(2)}, u32[]{:S(2)}) %collective-permute-start.8) | collective-permute-done | bytes 131104 | tf_op jit(solution)/shard_map/ppermute | solution.py:113
  51.2 1.6 %collective-permute-start.10 = (f32[128,1024]{1,0:T(8,128)S(1)}, f32[128,1024]{1,0:T(8,128)}, u32[]{:S(2)}, u32[]{:S(2)}) collective-permute-start(f32[128,1024]{1,0:T(8,128)S(1)} %collective-permute-done.3), channel_id=1, source_target_pairs={{0,16},{16,32},{32,48},{48,64},{64,80},{80,96},{96,112},{112,0},{1... | collective-permute-start | bytes 1572872 | tf_op jit(solution)/shard_map/ppermute | solution.py:130
  52.8 1.9 %collective-permute-start.11 = (f32[128,1024]{1,0:T(8,128)S(1)}, f32[128,1024]{1,0:T(8,128)S(1)}, u32[]{:S(2)}, u32[]{:S(2)}) collective-permute-start(f32[128,1024]{1,0:T(8,128)S(1)} %collective-permute-done.4), channel_id=1, source_target_pairs={{0,112},{16,0},{32,16},{48,32},{64,48},{80,64},{96,80},{112,96},{1... | collective-permute-start | bytes 1572872 | tf_op jit(solution)/shard_map/ppermute | solution.py:131
  57.3 1.8 %shard_map.60 = f32[8,8,8,128]{3,2,1,0:T(8,128)} custom-call(s32[8]{0:T(128)} %pattern_ref.3, s32[1]{0:T(128)} %bitcast.1.m_ref, f32[128,8,128]{2,1,0:T(8,128)} %copy-done.1), custom_call_target="tpu_custom_call" | custom-call | tf_op jit(solution)/shard_map/pallas_call | solution.py:147
  59.1 6.2 %all-to-all-start.1 = ((f32[8,64,128]{2,1,0:T(8,128)}), f32[8,64,128]{2,1,0:T(8,128)S(1)}, u32[]{:S(2)}, u32[]{:S(2)}) async-start(f32[8,64,128]{2,1,0:T(8,128)} %bitcast.99), calls=%async_computation.1 | async-start | bytes 524288 | tf_op jit(solution)/shard_map/all_to_all | solution.py:154
  65.3 2.0 %collective-permute-start.18 = (f32[128,1024]{1,0:T(8,128)}, f32[128,1024]{1,0:T(8,128)S(1)}, u32[]{:S(2)}, u32[]{:S(2)}) collective-permute-start(f32[128,1024]{1,0:T(8,128)} %collective-permute-done.10), channel_id=1, source_target_pairs={{0,16},{16,32},{32,48},{48,64},{64,80},{80,96},{96,112},{112,0},{1... | collective-permute-start | bytes 1572872 | tf_op jit(solution)/shard_map/ppermute | solution.py:130
  67.4 1.5 %collective-permute-start.19 = (f32[128,1024]{1,0:T(8,128)S(1)}, f32[128,1024]{1,0:T(8,128)S(1)}, u32[]{:S(2)}, u32[]{:S(2)}) collective-permute-start(f32[128,1024]{1,0:T(8,128)S(1)} %collective-permute-done.11), channel_id=1, source_target_pairs={{0,112},{16,0},{32,16},{48,32},{64,48},{80,64},{96,80},{112,96},{1... | collective-permute-start | bytes 1572872 | tf_op jit(solution)/shard_map/ppermute | solution.py:131
  68.9 1.9 %bitcast_dynamic-update-slice_fusion.3 = f32[8,128,1024]{2,1,0:T(8,128)} fusion(f32[8,128,1024]{2,1,0:T(8,128)} %bitcast_dynamic-update-slice_fusion.4, s32[]{:T(128)S(6)} %select_n.115, f32[128,1024]{1,0:T(8,128)} %collective-permute-done.10), kind=kLoop, calls=%fused_computation.3 | loop fusion | bytes 1048580 | tf_op jit(solution)/shard_map/dynamic_update_slice | solution.py:122
  71.6 5.7 %all-to-all-done.1 = f32[8,64,128]{2,1,0:T(8,128)S(1)} async-done(((f32[8,64,128]{2,1,0:T(8,128)}), f32[8,64,128]{2,1,0:T(8,128)S(1)}, u32[]{:S(2)}, u32[]{:S(2)}) %all-to-all-start.1) | async-done | bytes 262176 | tf_op jit(solution)/shard_map/all_to_all | solution.py:154
  78.1 2.4 %collective-permute-start.14 = (f32[256,128]{1,0:T(8,128)S(1)}, f32[256,128]{1,0:T(8,128)S(1)}, u32[]{:S(2)}, u32[]{:S(2)}) collective-permute-start(f32[256,128]{1,0:T(8,128)S(1)} %get-tuple-element.13), channel_id=1, source_target_pairs={{0,12},{4,0},{8,4},{12,8},{1,13},{5,1},{9,5},{13,9},{2,14},{6,2},{... | collective-permute-start | bytes 393224 | tf_op jit(solution)/shard_map/ppermute | solution.py:171
  80.5 1.0 collective-permute-start.13
  82.7 2.8 %collective-permute-start.21 = (f32[128,512]{1,0:T(8,128)S(1)}, f32[128,512]{1,0:T(8,128)S(1)}, u32[]{:S(2)}, u32[]{:S(2)}) collective-permute-start(f32[128,512]{1,0:T(8,128)S(1)} %slice.25), channel_id=1, source_target_pairs={{0,112},{16,0},{32,16},{48,32},{64,48},{80,64},{96,80},{112,96},{1... | collective-permute-start | bytes 786440 | tf_op jit(solution)/shard_map/ppermute | solution.py:136
  87.0 1.3 %collective-permute-done.12 = f32[256,128]{1,0:T(8,128)S(1)} collective-permute-done((f32[256,128]{1,0:T(8,128)S(1)}, f32[256,128]{1,0:T(8,128)S(1)}, u32[]{:S(2)}, u32[]{:S(2)}) %collective-permute-start.12) | collective-permute-done | bytes 131104 | tf_op jit(solution)/shard_map/ppermute | solution.py:171
  89.9 2.3 %collective-permute-start.16 = (f32[320,128]{1,0:T(8,128)S(1)}, f32[320,128]{1,0:T(8,128)S(1)}, u32[]{:S(2)}, u32[]{:S(2)}) collective-permute-start(f32[320,128]{1,0:T(8,128)S(1)} %pad_maximum_fusion), channel_id=1, source_target_pairs={{0,2},{1,3},{2,0},{3,1},{4,6},{5,7},{6,4},{7,5},{8,10},{9,11},{10,... | collective-permute-start | bytes 491528 | tf_op jit(solution)/shard_map/ppermute | solution.py:180
  92.2 0.9 collective-permute-start.17
  93.8 3.0 %collective-permute-done.16 = f32[320,128]{1,0:T(8,128)S(1)} collective-permute-done((f32[320,128]{1,0:T(8,128)S(1)}, f32[320,128]{1,0:T(8,128)S(1)}, u32[]{:S(2)}, u32[]{:S(2)}) %collective-permute-start.16) | collective-permute-done | bytes 163872 | tf_op jit(solution)/shard_map/ppermute | solution.py:180
  96.8 1.6 %collective-permute-done.17 = f32[320,128]{1,0:T(8,128)S(1)} collective-permute-done((f32[320,128]{1,0:T(8,128)S(1)}, f32[320,128]{1,0:T(8,128)S(1)}, u32[]{:S(2)}, u32[]{:S(2)}) %collective-permute-start.17) | collective-permute-done | bytes 163872 | tf_op jit(solution)/shard_map/ppermute | solution.py:180
  98.6 5.1 %shard_map.61 = (f32[32,1024]{1,0:T(8,128)}, f32[128,1024]{1,0:T(8,128)}) custom-call(s32[1]{0:T(128)} %bitcast.far_ref, f32[1024,128]{1,0:T(8,128)S(1)} %bitcast.88, f32[32,1024]{1,0:T(8,128)S(1)} %bitcast.89, f32[1024,1024]{1,0:T(8,128)} %bitcast.45.block_ref, f32[128,512]{1,0:T(8,128)S(1)} %collective-permute-done.20.left_ref, ...), custom_call_target="tpu_custom_call" | custom-call | tf_op jit(solution)/shard_map/pallas_call | solution.py:191
  (62 shorter events, 12.3 us)
Async XLA Ops:
  0.6 6.9 %collective-permute-start = (f32[32,1024]{1,0:T(8,128)}, f32[32,1024]{1,0:T(8,128)S(1)}, u32[]{:S(2)}, u32[]{:S(2)}) collective-permute-start(f32[32,1024]{1,0:T(8,128)} %param.6), channel_id=1, source_target_pairs={{0,4},{4,8},{8,12},{12,0},{1,5},{5,9},{9,13},{13,1},{2,6},{6,10},{... | collective-permute-start | bytes 393224 | tf_op jit(solution)/shard_map/ppermute | solution.py:82
  2.2 9.0 %collective-permute-start.1 = (f32[32,1024]{1,0:T(8,128)}, f32[32,1024]{1,0:T(8,128)S(1)}, u32[]{:S(2)}, u32[]{:S(2)}) collective-permute-start(f32[32,1024]{1,0:T(8,128)} %param.6), channel_id=1, source_target_pairs={{0,8},{4,12},{8,0},{12,4},{1,9},{5,13},{9,1},{13,5},{2,10},{6,14},... | collective-permute-start | bytes 393224 | tf_op jit(solution)/shard_map/ppermute | solution.py:82
  4.9 6.2 %collective-permute-start.2 = (f32[32,1024]{1,0:T(8,128)}, f32[32,1024]{1,0:T(8,128)S(1)}, u32[]{:S(2)}, u32[]{:S(2)}) collective-permute-start(f32[32,1024]{1,0:T(8,128)} %param.6), channel_id=1, source_target_pairs={{0,12},{4,0},{8,4},{12,8},{1,13},{5,1},{9,5},{13,9},{2,14},{6,2},{... | collective-permute-start | bytes 393224 | tf_op jit(solution)/shard_map/ppermute | solution.py:82
  12.1 25.7 %collective-permute-start.6 = (f32[32,512]{1,0:T(8,128)S(1)}, f32[32,512]{1,0:T(8,128)S(1)}, u32[]{:S(2)}, u32[]{:S(2)}) collective-permute-start(f32[32,512]{1,0:T(8,128)S(1)} %get-tuple-element.16), channel_id=1, source_target_pairs={{0,16},{1,48},{2,80},{3,112},{4,20},{5,52},{6,84},{7,116},{8,24},{... | collective-permute-start | bytes 196616 | tf_op jit(solution)/shard_map/ppermute | solution.py:106
  16.7 21.1 %collective-permute-start.5 = (f32[32,512]{1,0:T(8,128)S(1)}, f32[32,512]{1,0:T(8,128)S(1)}, u32[]{:S(2)}, u32[]{:S(2)}) collective-permute-start(f32[32,512]{1,0:T(8,128)S(1)} %get-tuple-element.15), channel_id=1, source_target_pairs={{0,0},{1,32},{2,64},{3,96},{4,4},{5,36},{6,68},{7,100},{8,8},{9,40... | collective-permute-start | bytes 196616 | tf_op jit(solution)/shard_map/ppermute | solution.py:102
  22.0 29.2 %collective-permute-start.3 = (f32[128,1024]{1,0:T(8,128)S(1)}, f32[128,1024]{1,0:T(8,128)S(1)}, u32[]{:S(2)}, u32[]{:S(2)}) collective-permute-start(f32[128,1024]{1,0:T(8,128)S(1)} %bitcast.93), channel_id=1, source_target_pairs={{0,16},{16,32},{32,48},{48,64},{64,80},{80,96},{96,112},{112,0},{1... | collective-permute-start | bytes 1572872 | tf_op jit(solution)/shard_map/ppermute | solution.py:130
  22.9 29.9 %collective-permute-start.4 = (f32[128,1024]{1,0:T(8,128)S(1)}, f32[128,1024]{1,0:T(8,128)S(1)}, u32[]{:S(2)}, u32[]{:S(2)}) collective-permute-start(f32[128,1024]{1,0:T(8,128)S(1)} %bitcast.94), channel_id=1, source_target_pairs={{0,112},{16,0},{32,16},{48,32},{64,48},{80,64},{96,80},{112,96},{1... | collective-permute-start | bytes 1572872 | tf_op jit(solution)/shard_map/ppermute | solution.py:131
  29.6 26.9 %all-to-all-start = ((f32[128,8,128]{2,1,0:T(8,128)}), f32[128,8,128]{2,1,0:T(8,128)S(1)}, u32[]{:S(2)}, u32[]{:S(2)}) async-start(f32[128,8,128]{2,1,0:T(8,128)} %bitcast.90), calls=%async_computation | async-start | bytes 1048576 | tf_op jit(solution)/shard_map/all_to_all | solution.py:146
  37.8 8.2 %collective-permute-start.7 = (f32[2,32,512]{2,1,0:T(8,128)S(1)}, f32[2,32,512]{2,1,0:T(8,128)S(1)}, u32[]{:S(2)}, u32[]{:S(2)}) collective-permute-start(f32[2,32,512]{2,1,0:T(8,128)S(1)} %maximum_select_fusion.1), channel_id=1, source_target_pairs={{0,1},{1,2},{2,3},{3,0},{4,5},{5,6},{6,7},{7,4},{8,9},{9,10},{10,1... | collective-permute-start | bytes 393224 | tf_op jit(solution)/shard_map/ppermute | solution.py:113
  42.7 8.4 %collective-permute-start.8 = (f32[2,32,512]{2,1,0:T(8,128)S(1)}, f32[2,32,512]{2,1,0:T(8,128)S(1)}, u32[]{:S(2)}, u32[]{:S(2)}) collective-permute-start(f32[2,32,512]{2,1,0:T(8,128)S(1)} %maximum_select_fusion.1), channel_id=1, source_target_pairs={{0,2},{1,3},{2,0},{3,1},{4,6},{5,7},{6,4},{7,5},{8,10},{9,11},{10,... | collective-permute-start | bytes 393224 | tf_op jit(solution)/shard_map/ppermute | solution.py:113
  44.2 10.4 %collective-permute-start.9 = (f32[2,32,512]{2,1,0:T(8,128)S(1)}, f32[2,32,512]{2,1,0:T(8,128)S(1)}, u32[]{:S(2)}, u32[]{:S(2)}) collective-permute-start(f32[2,32,512]{2,1,0:T(8,128)S(1)} %maximum_select_fusion.1), channel_id=1, source_target_pairs={{0,3},{1,0},{2,1},{3,2},{4,7},{5,4},{6,5},{7,6},{8,11},{9,8},{10,9... | collective-permute-start | bytes 393224 | tf_op jit(solution)/shard_map/ppermute | solution.py:113
  51.2 14.2 %collective-permute-start.10 = (f32[128,1024]{1,0:T(8,128)S(1)}, f32[128,1024]{1,0:T(8,128)}, u32[]{:S(2)}, u32[]{:S(2)}) collective-permute-start(f32[128,1024]{1,0:T(8,128)S(1)} %collective-permute-done.3), channel_id=1, source_target_pairs={{0,16},{16,32},{32,48},{48,64},{64,80},{80,96},{96,112},{112,0},{1... | collective-permute-start | bytes 1572872 | tf_op jit(solution)/shard_map/ppermute | solution.py:130
  52.8 14.6 %collective-permute-start.11 = (f32[128,1024]{1,0:T(8,128)S(1)}, f32[128,1024]{1,0:T(8,128)S(1)}, u32[]{:S(2)}, u32[]{:S(2)}) collective-permute-start(f32[128,1024]{1,0:T(8,128)S(1)} %collective-permute-done.4), channel_id=1, source_target_pairs={{0,112},{16,0},{32,16},{48,32},{64,48},{80,64},{96,80},{112,96},{1... | collective-permute-start | bytes 1572872 | tf_op jit(solution)/shard_map/ppermute | solution.py:131
  56.5 0.8 copy-start.1
  59.1 18.2 %all-to-all-start.1 = ((f32[8,64,128]{2,1,0:T(8,128)}), f32[8,64,128]{2,1,0:T(8,128)S(1)}, u32[]{:S(2)}, u32[]{:S(2)}) async-start(f32[8,64,128]{2,1,0:T(8,128)} %bitcast.99), calls=%async_computation.1 | async-start | bytes 524288 | tf_op jit(solution)/shard_map/all_to_all | solution.py:154
  65.3 16.7 %collective-permute-start.18 = (f32[128,1024]{1,0:T(8,128)}, f32[128,1024]{1,0:T(8,128)S(1)}, u32[]{:S(2)}, u32[]{:S(2)}) collective-permute-start(f32[128,1024]{1,0:T(8,128)} %collective-permute-done.10), channel_id=1, source_target_pairs={{0,16},{16,32},{32,48},{48,64},{64,80},{80,96},{96,112},{112,0},{1... | collective-permute-start | bytes 1572872 | tf_op jit(solution)/shard_map/ppermute | solution.py:130
  67.4 15.3 %collective-permute-start.19 = (f32[128,1024]{1,0:T(8,128)S(1)}, f32[128,1024]{1,0:T(8,128)S(1)}, u32[]{:S(2)}, u32[]{:S(2)}) collective-permute-start(f32[128,1024]{1,0:T(8,128)S(1)} %collective-permute-done.11), channel_id=1, source_target_pairs={{0,112},{16,0},{32,16},{48,32},{64,48},{80,64},{96,80},{112,96},{1... | collective-permute-start | bytes 1572872 | tf_op jit(solution)/shard_map/ppermute | solution.py:131
  78.0 20.6 %copy-start = (f32[128,1024]{1,0:T(8,128)S(1)}, f32[128,1024]{1,0:T(8,128)}, u32[]{:S(2)}) copy-start(f32[128,1024]{1,0:T(8,128)} %inverse_ref.1) | copy-start | bytes 1572868
  78.1 8.2 %collective-permute-start.14 = (f32[256,128]{1,0:T(8,128)S(1)}, f32[256,128]{1,0:T(8,128)S(1)}, u32[]{:S(2)}, u32[]{:S(2)}) collective-permute-start(f32[256,128]{1,0:T(8,128)S(1)} %get-tuple-element.13), channel_id=1, source_target_pairs={{0,12},{4,0},{8,4},{12,8},{1,13},{5,1},{9,5},{13,9},{2,14},{6,2},{... | collective-permute-start | bytes 393224 | tf_op jit(solution)/shard_map/ppermute | solution.py:171
  80.5 6.5 %collective-permute-start.13 = (f32[256,128]{1,0:T(8,128)S(1)}, f32[256,128]{1,0:T(8,128)S(1)}, u32[]{:S(2)}, u32[]{:S(2)}) collective-permute-start(f32[256,128]{1,0:T(8,128)S(1)} %get-tuple-element.14), channel_id=1, source_target_pairs={{0,8},{4,12},{8,0},{12,4},{1,9},{5,13},{9,1},{13,5},{2,10},{6,14},... | collective-permute-start | bytes 393224 | tf_op jit(solution)/shard_map/ppermute | solution.py:171
  81.5 6.9 %collective-permute-start.12 = (f32[256,128]{1,0:T(8,128)S(1)}, f32[256,128]{1,0:T(8,128)S(1)}, u32[]{:S(2)}, u32[]{:S(2)}) collective-permute-start(f32[256,128]{1,0:T(8,128)S(1)} %get-tuple-element.12), channel_id=1, source_target_pairs={{0,4},{4,8},{8,12},{12,0},{1,5},{5,9},{9,13},{13,1},{2,6},{6,10},{... | collective-permute-start | bytes 393224 | tf_op jit(solution)/shard_map/ppermute | solution.py:171
  82.0 16.5 %collective-permute-start.20 = (f32[128,512]{1,0:T(8,128)S(1)}, f32[128,512]{1,0:T(8,128)S(1)}, u32[]{:S(2)}, u32[]{:S(2)}) collective-permute-start(f32[128,512]{1,0:T(8,128)S(1)} %slice.24), channel_id=1, source_target_pairs={{0,16},{16,32},{32,48},{48,64},{64,80},{80,96},{96,112},{112,0},{1... | collective-permute-start | bytes 786440 | tf_op jit(solution)/shard_map/ppermute | solution.py:135
  82.7 15.9 %collective-permute-start.21 = (f32[128,512]{1,0:T(8,128)S(1)}, f32[128,512]{1,0:T(8,128)S(1)}, u32[]{:S(2)}, u32[]{:S(2)}) collective-permute-start(f32[128,512]{1,0:T(8,128)S(1)} %slice.25), channel_id=1, source_target_pairs={{0,112},{16,0},{32,16},{48,32},{64,48},{80,64},{96,80},{112,96},{1... | collective-permute-start | bytes 786440 | tf_op jit(solution)/shard_map/ppermute | solution.py:136
  88.4 5.4 %collective-permute-start.15 = (f32[320,128]{1,0:T(8,128)S(1)}, f32[320,128]{1,0:T(8,128)S(1)}, u32[]{:S(2)}, u32[]{:S(2)}) collective-permute-start(f32[320,128]{1,0:T(8,128)S(1)} %pad_maximum_fusion), channel_id=1, source_target_pairs={{0,1},{1,2},{2,3},{3,0},{4,5},{5,6},{6,7},{7,4},{8,9},{9,10},{10,1... | collective-permute-start | bytes 491528 | tf_op jit(solution)/shard_map/ppermute | solution.py:180
  89.9 6.9 %collective-permute-start.16 = (f32[320,128]{1,0:T(8,128)S(1)}, f32[320,128]{1,0:T(8,128)S(1)}, u32[]{:S(2)}, u32[]{:S(2)}) collective-permute-start(f32[320,128]{1,0:T(8,128)S(1)} %pad_maximum_fusion), channel_id=1, source_target_pairs={{0,2},{1,3},{2,0},{3,1},{4,6},{5,7},{6,4},{7,5},{8,10},{9,11},{10,... | collective-permute-start | bytes 491528 | tf_op jit(solution)/shard_map/ppermute | solution.py:180
  92.2 6.2 %collective-permute-start.17 = (f32[320,128]{1,0:T(8,128)S(1)}, f32[320,128]{1,0:T(8,128)S(1)}, u32[]{:S(2)}, u32[]{:S(2)}) collective-permute-start(f32[320,128]{1,0:T(8,128)S(1)} %pad_maximum_fusion), channel_id=1, source_target_pairs={{0,3},{1,0},{2,1},{3,2},{4,7},{5,4},{6,5},{7,6},{8,11},{9,8},{10,9... | collective-permute-start | bytes 491528 | tf_op jit(solution)/shard_map/ppermute | solution.py:180

commit v5 on v4

--- a/solution.py
+++ b/solution.py
@@ -40,26 +40,27 @@
 
 def last_kernel(
     far_ref, product_ref, rows_ref, block_ref, left_ref, right_ref, inverse_ref,
-    coupling_ref, out_ref, hi, lo,
+    coupling_ref, out_ref, halves,
 ):
     @pl.when(pl.program_id(0) == 0)
     def _():
         left = jnp.concatenate([product_ref[...].T, -rows_ref[...]], axis=0)
         high = left.astype(jnp.bfloat16)
-        hi[...] = high
-        lo[...] = (left - high.astype(jnp.float32)).astype(jnp.bfloat16)
+        halves[: B + 32] = high
+        halves[B + 32 :] = (left - high.astype(jnp.float32)).astype(jnp.bfloat16)
 
     def dot(a, b):
         return jnp.dot(a, b, preferred_element_type=jnp.float32)
 
-    def dot3(a_high, a_low, block):
+    def dot3(a, block):
         high = block.astype(jnp.bfloat16)
         low = (block - high.astype(jnp.float32)).astype(jnp.bfloat16)
-        return dot(a_high, low) + dot(a_low, high) + dot(a_high, high)
+        both = dot(a, high)
+        return dot(a[: B + 32], low) + both[B + 32 :] + both[: B + 32]
 
     far = pl.ds(pl.multiple_of(far_ref[0] * B, B), B)
     half = jnp.where(pl.program_id(0) < 2, left_ref[...], right_ref[...])
-    total = dot3(hi[...], lo[...], block_ref[...]) + dot3(hi[:, far], lo[:, far], half)
+    total = dot3(halves[...], block_ref[...]) + dot3(halves[:, far], half)
     out_ref[...] = inverse_ref[...] + total[:B]
     coupling_ref[...] = total[B:]
 
@@ -205,7 +206,7 @@
             columns(B),
         ],
         out_specs=[columns(32), columns(B)],
-        scratch_shapes=[pltpu.VMEM((B + 32, 1024), jnp.bfloat16)] * 2,
+        scratch_shapes=[pltpu.VMEM((2 * (B + 32), 1024), jnp.bfloat16)],
         compiler_params=pltpu.CompilerParams(vmem_limit_bytes=32 * 1024 * 1024),
     )(opposite, product, picked_rows, gathered, left, right, child_inverse)
 

time: 104 us -> 104 us (level)
  no operation moved by 1% of the time
where the time goes in v5:
time: 104 us
  starting transfers between devices  58.6 us (56%)
  waiting for transfers between devices  21.9 us (21%)
  local copies, waits for them, and re-layouts  11.8 us (11%)
  Pallas kernels  8.78 us (8%)
    ppermute x3, starting transfers between devices, shards(): down = lax.ppermute(down, 'z', shift_perm(NZ, -1))  10.1 us
    all_to_all x1, starting transfers between devices, shards(): cut = lax.all_to_all(listed, ('z', 'x', 'col'), 0, 0, tiled=True)  8.16 us
    dynamic_update_slice x7, local copies, waits for them, and re-layouts, place(): lax.dynamic_update_slice(whole, part[None], (lax.rem(z + 2 * NZ - d, NZ),...  6.93 us
    all_to_all x1, starting transfers between devices, shards(): wide = lax.all_to_all(wide, 'z', 0, 0, tiled=True)  6.21 us
    ppermute x3, starting transfers between devices, shards(): lax.ppermute(child_rows, 'x', shift_perm(NX, d))  5.73 us
    all_to_all x1, waiting for transfers between devices, shards(): wide = lax.all_to_all(wide, 'z', 0, 0, tiled=True)  5.71 us
    ppermute x3, waiting for transfers between devices, shards(): got = both if d == 0 else lax.ppermute(both, 'col', shift_perm(NY, d))  5.18 us
    ppermute x3, waiting for transfers between devices, shards(): got = pair if d == 0 else lax.ppermute(pair, 'col', shift_perm(NY, d))  5.08 us
  transfers between devices with their start and end apart: 24, of which 9 were waited for; matrix products, arithmetic and copies ran while one was open for 11% of the time, Pallas kernels for 4%

profile of v5, /device:TPU:8, one launch (start us, length us, event | category | flops | bytes accessed | tf_op | source)
XLA Modules:
  0.0 103.7 jit_solution(14849016994080129414)
XLA Ops:
  0.6 1.6 %collective-permute-start = (f32[32,1024]{1,0:T(8,128)}, f32[32,1024]{1,0:T(8,128)S(1)}, u32[]{:S(2)}, u32[]{:S(2)}) collective-permute-start(f32[32,1024]{1,0:T(8,128)} %param.6), channel_id=1, source_target_pairs={{0,4},{4,8},{8,12},{12,0},{1,5},{5,9},{9,13},{13,1},{2,6},{6,10},{... | collective-permute-start | bytes 393224 | tf_op jit(solution)/shard_map/ppermute | solution.py:83
  2.2 2.7 %collective-permute-start.1 = (f32[32,1024]{1,0:T(8,128)}, f32[32,1024]{1,0:T(8,128)S(1)}, u32[]{:S(2)}, u32[]{:S(2)}) collective-permute-start(f32[32,1024]{1,0:T(8,128)} %param.6), channel_id=1, source_target_pairs={{0,8},{4,12},{8,0},{12,4},{1,9},{5,13},{9,1},{13,5},{2,10},{6,14},... | collective-permute-start | bytes 393224 | tf_op jit(solution)/shard_map/ppermute | solution.py:83
  4.9 1.4 %collective-permute-start.2 = (f32[32,1024]{1,0:T(8,128)}, f32[32,1024]{1,0:T(8,128)S(1)}, u32[]{:S(2)}, u32[]{:S(2)}) collective-permute-start(f32[32,1024]{1,0:T(8,128)} %param.6), channel_id=1, source_target_pairs={{0,12},{4,0},{8,4},{12,8},{1,13},{5,1},{9,5},{13,9},{2,14},{6,2},{... | collective-permute-start | bytes 393224 | tf_op jit(solution)/shard_map/ppermute | solution.py:83
  6.4 0.9 bitcast_dynamic-update-slice_fusion.17
  7.5 3.6 %collective-permute-done.1 = f32[32,1024]{1,0:T(8,128)S(1)} collective-permute-done((f32[32,1024]{1,0:T(8,128)}, f32[32,1024]{1,0:T(8,128)S(1)}, u32[]{:S(2)}, u32[]{:S(2)}) %collective-permute-start.1) | collective-permute-done | bytes 131104 | tf_op jit(solution)/shard_map/ppermute | solution.py:83
  12.1 4.6 %collective-permute-start.6 = (f32[32,512]{1,0:T(8,128)S(1)}, f32[32,512]{1,0:T(8,128)S(1)}, u32[]{:S(2)}, u32[]{:S(2)}) collective-permute-start(f32[32,512]{1,0:T(8,128)S(1)} %get-tuple-element.16), channel_id=1, source_target_pairs={{0,16},{1,48},{2,80},{3,112},{4,20},{5,52},{6,84},{7,116},{8,24},{... | collective-permute-start | bytes 196616 | tf_op jit(solution)/shard_map/ppermute | solution.py:107
  16.7 3.3 %collective-permute-start.5 = (f32[32,512]{1,0:T(8,128)S(1)}, f32[32,512]{1,0:T(8,128)S(1)}, u32[]{:S(2)}, u32[]{:S(2)}) collective-permute-start(f32[32,512]{1,0:T(8,128)S(1)} %get-tuple-element.15), channel_id=1, source_target_pairs={{0,0},{1,32},{2,64},{3,96},{4,4},{5,36},{6,68},{7,100},{8,8},{9,40... | collective-permute-start | bytes 196616 | tf_op jit(solution)/shard_map/ppermute | solution.py:103
  20.0 1.9 %shard_map.59 = f32[2,4,4,4,8,128]{5,4,3,2,1,0:T(8,128)} custom-call(s32[8]{0:T(128)} %pattern_ref.3, s32[1]{0:T(128)} %bitcast.2.y_ref, f32[128,1024]{1,0:T(8,128)} %root_ref.1), custom_call_target="tpu_custom_call" | custom-call | tf_op jit(solution)/shard_map/pallas_call | solution.py:140
  22.9 6.8 %collective-permute-start.4 = (f32[128,1024]{1,0:T(8,128)S(1)}, f32[128,1024]{1,0:T(8,128)S(1)}, u32[]{:S(2)}, u32[]{:S(2)}) collective-permute-start(f32[128,1024]{1,0:T(8,128)S(1)} %bitcast.94), channel_id=1, source_target_pairs={{0,112},{16,0},{32,16},{48,32},{64,48},{80,64},{96,80},{112,96},{1... | collective-permute-start | bytes 1572872 | tf_op jit(solution)/shard_map/ppermute | solution.py:132
  29.6 8.2 %all-to-all-start = ((f32[128,8,128]{2,1,0:T(8,128)}), f32[128,8,128]{2,1,0:T(8,128)S(1)}, u32[]{:S(2)}, u32[]{:S(2)}) async-start(f32[128,8,128]{2,1,0:T(8,128)} %bitcast.90), calls=%async_computation | async-start | bytes 1048576 | tf_op jit(solution)/shard_map/all_to_all | solution.py:147
  37.8 1.5 %collective-permute-start.7 = (f32[2,32,512]{2,1,0:T(8,128)S(1)}, f32[2,32,512]{2,1,0:T(8,128)S(1)}, u32[]{:S(2)}, u32[]{:S(2)}) collective-permute-start(f32[2,32,512]{2,1,0:T(8,128)S(1)} %maximum_select_fusion.1), channel_id=1, source_target_pairs={{0,1},{1,2},{2,3},{3,0},{4,5},{5,6},{6,7},{7,4},{8,9},{9,10},{10,1... | collective-permute-start | bytes 393224 | tf_op jit(solution)/shard_map/ppermute | solution.py:114
  39.4 2.5 %broadcast_in_dim.78 = f32[8,128,1024]{2,1,0:T(8,128)} broadcast(f32[]{:T(128)} %constant.104.clone.1), dimensions={} | broadcast | bytes 4194308 | tf_op jit(solution)/shard_map/broadcast_in_dim | solution.py:120
  42.7 1.5 %collective-permute-start.8 = (f32[2,32,512]{2,1,0:T(8,128)S(1)}, f32[2,32,512]{2,1,0:T(8,128)S(1)}, u32[]{:S(2)}, u32[]{:S(2)}) collective-permute-start(f32[2,32,512]{2,1,0:T(8,128)S(1)} %maximum_select_fusion.1), channel_id=1, source_target_pairs={{0,2},{1,3},{2,0},{3,1},{4,6},{5,7},{6,4},{7,5},{8,10},{9,11},{10,... | collective-permute-start | bytes 393224 | tf_op jit(solution)/shard_map/ppermute | solution.py:114
  44.2 1.7 %collective-permute-start.9 = (f32[2,32,512]{2,1,0:T(8,128)S(1)}, f32[2,32,512]{2,1,0:T(8,128)S(1)}, u32[]{:S(2)}, u32[]{:S(2)}) collective-permute-start(f32[2,32,512]{2,1,0:T(8,128)S(1)} %maximum_select_fusion.1), channel_id=1, source_target_pairs={{0,3},{1,0},{2,1},{3,2},{4,7},{5,4},{6,5},{7,6},{8,11},{9,8},{10,9... | collective-permute-start | bytes 393224 | tf_op jit(solution)/shard_map/ppermute | solution.py:114
  46.1 5.1 %collective-permute-done.8 = f32[2,32,512]{2,1,0:T(8,128)S(1)} collective-permute-done((f32[2,32,512]{2,1,0:T(8,128)S(1)}, f32[2,32,512]{2,1,0:T(8,128)S(1)}, u32[]{:S(2)}, u32[]{:S(2)}) %collective-permute-start.8) | collective-permute-done | bytes 131104 | tf_op jit(solution)/shard_map/ppermute | solution.py:114
  51.2 1.6 %collective-permute-start.10 = (f32[128,1024]{1,0:T(8,128)S(1)}, f32[128,1024]{1,0:T(8,128)}, u32[]{:S(2)}, u32[]{:S(2)}) collective-permute-start(f32[128,1024]{1,0:T(8,128)S(1)} %collective-permute-done.3), channel_id=1, source_target_pairs={{0,16},{16,32},{32,48},{48,64},{64,80},{80,96},{96,112},{112,0},{1... | collective-permute-start | bytes 1572872 | tf_op jit(solution)/shard_map/ppermute | solution.py:131
  52.8 1.9 %collective-permute-start.11 = (f32[128,1024]{1,0:T(8,128)S(1)}, f32[128,1024]{1,0:T(8,128)S(1)}, u32[]{:S(2)}, u32[]{:S(2)}) collective-permute-start(f32[128,1024]{1,0:T(8,128)S(1)} %collective-permute-done.4), channel_id=1, source_target_pairs={{0,112},{16,0},{32,16},{48,32},{64,48},{80,64},{96,80},{112,96},{1... | collective-permute-start | bytes 1572872 | tf_op jit(solution)/shard_map/ppermute | solution.py:132
  57.3 1.8 %shard_map.60 = f32[8,8,8,128]{3,2,1,0:T(8,128)} custom-call(s32[8]{0:T(128)} %pattern_ref.3, s32[1]{0:T(128)} %bitcast.1.m_ref, f32[128,8,128]{2,1,0:T(8,128)} %copy-done.1), custom_call_target="tpu_custom_call" | custom-call | tf_op jit(solution)/shard_map/pallas_call | solution.py:148
  59.1 6.2 %all-to-all-start.1 = ((f32[8,64,128]{2,1,0:T(8,128)}), f32[8,64,128]{2,1,0:T(8,128)S(1)}, u32[]{:S(2)}, u32[]{:S(2)}) async-start(f32[8,64,128]{2,1,0:T(8,128)} %bitcast.99), calls=%async_computation.1 | async-start | bytes 524288 | tf_op jit(solution)/shard_map/all_to_all | solution.py:155
  65.3 2.0 %collective-permute-start.18 = (f32[128,1024]{1,0:T(8,128)}, f32[128,1024]{1,0:T(8,128)S(1)}, u32[]{:S(2)}, u32[]{:S(2)}) collective-permute-start(f32[128,1024]{1,0:T(8,128)} %collective-permute-done.10), channel_id=1, source_target_pairs={{0,16},{16,32},{32,48},{48,64},{64,80},{80,96},{96,112},{112,0},{1... | collective-permute-start | bytes 1572872 | tf_op jit(solution)/shard_map/ppermute | solution.py:131
  67.4 1.5 %collective-permute-start.19 = (f32[128,1024]{1,0:T(8,128)S(1)}, f32[128,1024]{1,0:T(8,128)S(1)}, u32[]{:S(2)}, u32[]{:S(2)}) collective-permute-start(f32[128,1024]{1,0:T(8,128)S(1)} %collective-permute-done.11), channel_id=1, source_target_pairs={{0,112},{16,0},{32,16},{48,32},{64,48},{80,64},{96,80},{112,96},{1... | collective-permute-start | bytes 1572872 | tf_op jit(solution)/shard_map/ppermute | solution.py:132
  68.9 1.9 %bitcast_dynamic-update-slice_fusion.3 = f32[8,128,1024]{2,1,0:T(8,128)} fusion(f32[8,128,1024]{2,1,0:T(8,128)} %bitcast_dynamic-update-slice_fusion.4, s32[]{:T(128)S(6)} %select_n.115, f32[128,1024]{1,0:T(8,128)} %collective-permute-done.10), kind=kLoop, calls=%fused_computation.3 | loop fusion | bytes 1048580 | tf_op jit(solution)/shard_map/dynamic_update_slice | solution.py:123
  71.6 5.7 %all-to-all-done.1 = f32[8,64,128]{2,1,0:T(8,128)S(1)} async-done(((f32[8,64,128]{2,1,0:T(8,128)}), f32[8,64,128]{2,1,0:T(8,128)S(1)}, u32[]{:S(2)}, u32[]{:S(2)}) %all-to-all-start.1) | async-done | bytes 262176 | tf_op jit(solution)/shard_map/all_to_all | solution.py:155
  78.1 2.4 %collective-permute-start.14 = (f32[256,128]{1,0:T(8,128)S(1)}, f32[256,128]{1,0:T(8,128)S(1)}, u32[]{:S(2)}, u32[]{:S(2)}) collective-permute-start(f32[256,128]{1,0:T(8,128)S(1)} %get-tuple-element.13), channel_id=1, source_target_pairs={{0,12},{4,0},{8,4},{12,8},{1,13},{5,1},{9,5},{13,9},{2,14},{6,2},{... | collective-permute-start | bytes 393224 | tf_op jit(solution)/shard_map/ppermute | solution.py:172
  80.5 1.0 collective-permute-start.13
  82.7 2.8 %collective-permute-start.21 = (f32[128,512]{1,0:T(8,128)S(1)}, f32[128,512]{1,0:T(8,128)S(1)}, u32[]{:S(2)}, u32[]{:S(2)}) collective-permute-start(f32[128,512]{1,0:T(8,128)S(1)} %slice.25), channel_id=1, source_target_pairs={{0,112},{16,0},{32,16},{48,32},{64,48},{80,64},{96,80},{112,96},{1... | collective-permute-start | bytes 786440 | tf_op jit(solution)/shard_map/ppermute | solution.py:137
  87.0 1.3 %collective-permute-done.12 = f32[256,128]{1,0:T(8,128)S(1)} collective-permute-done((f32[256,128]{1,0:T(8,128)S(1)}, f32[256,128]{1,0:T(8,128)S(1)}, u32[]{:S(2)}, u32[]{:S(2)}) %collective-permute-start.12) | collective-permute-done | bytes 131104 | tf_op jit(solution)/shard_map/ppermute | solution.py:172
  89.9 2.3 %collective-permute-start.16 = (f32[320,128]{1,0:T(8,128)S(1)}, f32[320,128]{1,0:T(8,128)S(1)}, u32[]{:S(2)}, u32[]{:S(2)}) collective-permute-start(f32[320,128]{1,0:T(8,128)S(1)} %pad_maximum_fusion), channel_id=1, source_target_pairs={{0,2},{1,3},{2,0},{3,1},{4,6},{5,7},{6,4},{7,5},{8,10},{9,11},{10,... | collective-permute-start | bytes 491528 | tf_op jit(solution)/shard_map/ppermute | solution.py:181
  92.2 0.9 collective-permute-start.17
  93.8 3.0 %collective-permute-done.16 = f32[320,128]{1,0:T(8,128)S(1)} collective-permute-done((f32[320,128]{1,0:T(8,128)S(1)}, f32[320,128]{1,0:T(8,128)S(1)}, u32[]{:S(2)}, u32[]{:S(2)}) %collective-permute-start.16) | collective-permute-done | bytes 163872 | tf_op jit(solution)/shard_map/ppermute | solution.py:181
  96.8 1.6 %collective-permute-done.17 = f32[320,128]{1,0:T(8,128)S(1)} collective-permute-done((f32[320,128]{1,0:T(8,128)S(1)}, f32[320,128]{1,0:T(8,128)S(1)}, u32[]{:S(2)}, u32[]{:S(2)}) %collective-permute-start.17) | collective-permute-done | bytes 163872 | tf_op jit(solution)/shard_map/ppermute | solution.py:181
  98.6 5.1 %shard_map.61 = (f32[32,1024]{1,0:T(8,128)}, f32[128,1024]{1,0:T(8,128)}) custom-call(s32[1]{0:T(128)} %bitcast.far_ref, f32[1024,128]{1,0:T(8,128)S(1)} %bitcast.88, f32[32,1024]{1,0:T(8,128)S(1)} %bitcast.89, f32[1024,1024]{1,0:T(8,128)} %bitcast.45.block_ref, f32[128,512]{1,0:T(8,128)S(1)} %collective-permute-done.20.left_ref, ...), custom_call_target="tpu_custom_call" | custom-call | tf_op jit(solution)/shard_map/pallas_call | solution.py:192
  (62 shorter events, 12.3 us)
Async XLA Ops:
  0.6 6.9 %collective-permute-start = (f32[32,1024]{1,0:T(8,128)}, f32[32,1024]{1,0:T(8,128)S(1)}, u32[]{:S(2)}, u32[]{:S(2)}) collective-permute-start(f32[32,1024]{1,0:T(8,128)} %param.6), channel_id=1, source_target_pairs={{0,4},{4,8},{8,12},{12,0},{1,5},{5,9},{9,13},{13,1},{2,6},{6,10},{... | collective-permute-start | bytes 393224 | tf_op jit(solution)/shard_map/ppermute | solution.py:83
  2.2 9.0 %collective-permute-start.1 = (f32[32,1024]{1,0:T(8,128)}, f32[32,1024]{1,0:T(8,128)S(1)}, u32[]{:S(2)}, u32[]{:S(2)}) collective-permute-start(f32[32,1024]{1,0:T(8,128)} %param.6), channel_id=1, source_target_pairs={{0,8},{4,12},{8,0},{12,4},{1,9},{5,13},{9,1},{13,5},{2,10},{6,14},... | collective-permute-start | bytes 393224 | tf_op jit(solution)/shard_map/ppermute | solution.py:83
  4.9 6.2 %collective-permute-start.2 = (f32[32,1024]{1,0:T(8,128)}, f32[32,1024]{1,0:T(8,128)S(1)}, u32[]{:S(2)}, u32[]{:S(2)}) collective-permute-start(f32[32,1024]{1,0:T(8,128)} %param.6), channel_id=1, source_target_pairs={{0,12},{4,0},{8,4},{12,8},{1,13},{5,1},{9,5},{13,9},{2,14},{6,2},{... | collective-permute-start | bytes 393224 | tf_op jit(solution)/shard_map/ppermute | solution.py:83
  12.1 25.7 %collective-permute-start.6 = (f32[32,512]{1,0:T(8,128)S(1)}, f32[32,512]{1,0:T(8,128)S(1)}, u32[]{:S(2)}, u32[]{:S(2)}) collective-permute-start(f32[32,512]{1,0:T(8,128)S(1)} %get-tuple-element.16), channel_id=1, source_target_pairs={{0,16},{1,48},{2,80},{3,112},{4,20},{5,52},{6,84},{7,116},{8,24},{... | collective-permute-start | bytes 196616 | tf_op jit(solution)/shard_map/ppermute | solution.py:107
  16.7 21.1 %collective-permute-start.5 = (f32[32,512]{1,0:T(8,128)S(1)}, f32[32,512]{1,0:T(8,128)S(1)}, u32[]{:S(2)}, u32[]{:S(2)}) collective-permute-start(f32[32,512]{1,0:T(8,128)S(1)} %get-tuple-element.15), channel_id=1, source_target_pairs={{0,0},{1,32},{2,64},{3,96},{4,4},{5,36},{6,68},{7,100},{8,8},{9,40... | collective-permute-start | bytes 196616 | tf_op jit(solution)/shard_map/ppermute | solution.py:103
  22.0 29.2 %collective-permute-start.3 = (f32[128,1024]{1,0:T(8,128)S(1)}, f32[128,1024]{1,0:T(8,128)S(1)}, u32[]{:S(2)}, u32[]{:S(2)}) collective-permute-start(f32[128,1024]{1,0:T(8,128)S(1)} %bitcast.93), channel_id=1, source_target_pairs={{0,16},{16,32},{32,48},{48,64},{64,80},{80,96},{96,112},{112,0},{1... | collective-permute-start | bytes 1572872 | tf_op jit(solution)/shard_map/ppermute | solution.py:131
  22.9 29.9 %collective-permute-start.4 = (f32[128,1024]{1,0:T(8,128)S(1)}, f32[128,1024]{1,0:T(8,128)S(1)}, u32[]{:S(2)}, u32[]{:S(2)}) collective-permute-start(f32[128,1024]{1,0:T(8,128)S(1)} %bitcast.94), channel_id=1, source_target_pairs={{0,112},{16,0},{32,16},{48,32},{64,48},{80,64},{96,80},{112,96},{1... | collective-permute-start | bytes 1572872 | tf_op jit(solution)/shard_map/ppermute | solution.py:132
  29.6 26.9 %all-to-all-start = ((f32[128,8,128]{2,1,0:T(8,128)}), f32[128,8,128]{2,1,0:T(8,128)S(1)}, u32[]{:S(2)}, u32[]{:S(2)}) async-start(f32[128,8,128]{2,1,0:T(8,128)} %bitcast.90), calls=%async_computation | async-start | bytes 1048576 | tf_op jit(solution)/shard_map/all_to_all | solution.py:147
  37.8 8.2 %collective-permute-start.7 = (f32[2,32,512]{2,1,0:T(8,128)S(1)}, f32[2,32,512]{2,1,0:T(8,128)S(1)}, u32[]{:S(2)}, u32[]{:S(2)}) collective-permute-start(f32[2,32,512]{2,1,0:T(8,128)S(1)} %maximum_select_fusion.1), channel_id=1, source_target_pairs={{0,1},{1,2},{2,3},{3,0},{4,5},{5,6},{6,7},{7,4},{8,9},{9,10},{10,1... | collective-permute-start | bytes 393224 | tf_op jit(solution)/shard_map/ppermute | solution.py:114
  42.7 8.4 %collective-permute-start.8 = (f32[2,32,512]{2,1,0:T(8,128)S(1)}, f32[2,32,512]{2,1,0:T(8,128)S(1)}, u32[]{:S(2)}, u32[]{:S(2)}) collective-permute-start(f32[2,32,512]{2,1,0:T(8,128)S(1)} %maximum_select_fusion.1), channel_id=1, source_target_pairs={{0,2},{1,3},{2,0},{3,1},{4,6},{5,7},{6,4},{7,5},{8,10},{9,11},{10,... | collective-permute-start | bytes 393224 | tf_op jit(solution)/shard_map/ppermute | solution.py:114
  44.2 10.4 %collective-permute-start.9 = (f32[2,32,512]{2,1,0:T(8,128)S(1)}, f32[2,32,512]{2,1,0:T(8,128)S(1)}, u32[]{:S(2)}, u32[]{:S(2)}) collective-permute-start(f32[2,32,512]{2,1,0:T(8,128)S(1)} %maximum_select_fusion.1), channel_id=1, source_target_pairs={{0,3},{1,0},{2,1},{3,2},{4,7},{5,4},{6,5},{7,6},{8,11},{9,8},{10,9... | collective-permute-start | bytes 393224 | tf_op jit(solution)/shard_map/ppermute | solution.py:114
  51.2 14.2 %collective-permute-start.10 = (f32[128,1024]{1,0:T(8,128)S(1)}, f32[128,1024]{1,0:T(8,128)}, u32[]{:S(2)}, u32[]{:S(2)}) collective-permute-start(f32[128,1024]{1,0:T(8,128)S(1)} %collective-permute-done.3), channel_id=1, source_target_pairs={{0,16},{16,32},{32,48},{48,64},{64,80},{80,96},{96,112},{112,0},{1... | collective-permute-start | bytes 1572872 | tf_op jit(solution)/shard_map/ppermute | solution.py:131
  52.8 14.6 %collective-permute-start.11 = (f32[128,1024]{1,0:T(8,128)S(1)}, f32[128,1024]{1,0:T(8,128)S(1)}, u32[]{:S(2)}, u32[]{:S(2)}) collective-permute-start(f32[128,1024]{1,0:T(8,128)S(1)} %collective-permute-done.4), channel_id=1, source_target_pairs={{0,112},{16,0},{32,16},{48,32},{64,48},{80,64},{96,80},{112,96},{1... | collective-permute-start | bytes 1572872 | tf_op jit(solution)/shard_map/ppermute | solution.py:132
  56.5 0.8 copy-start.1
  59.1 18.2 %all-to-all-start.1 = ((f32[8,64,128]{2,1,0:T(8,128)}), f32[8,64,128]{2,1,0:T(8,128)S(1)}, u32[]{:S(2)}, u32[]{:S(2)}) async-start(f32[8,64,128]{2,1,0:T(8,128)} %bitcast.99), calls=%async_computation.1 | async-start | bytes 524288 | tf_op jit(solution)/shard_map/all_to_all | solution.py:155
  65.3 16.7 %collective-permute-start.18 = (f32[128,1024]{1,0:T(8,128)}, f32[128,1024]{1,0:T(8,128)S(1)}, u32[]{:S(2)}, u32[]{:S(2)}) collective-permute-start(f32[128,1024]{1,0:T(8,128)} %collective-permute-done.10), channel_id=1, source_target_pairs={{0,16},{16,32},{32,48},{48,64},{64,80},{80,96},{96,112},{112,0},{1... | collective-permute-start | bytes 1572872 | tf_op jit(solution)/shard_map/ppermute | solution.py:131
  67.4 15.3 %collective-permute-start.19 = (f32[128,1024]{1,0:T(8,128)S(1)}, f32[128,1024]{1,0:T(8,128)S(1)}, u32[]{:S(2)}, u32[]{:S(2)}) collective-permute-start(f32[128,1024]{1,0:T(8,128)S(1)} %collective-permute-done.11), channel_id=1, source_target_pairs={{0,112},{16,0},{32,16},{48,32},{64,48},{80,64},{96,80},{112,96},{1... | collective-permute-start | bytes 1572872 | tf_op jit(solution)/shard_map/ppermute | solution.py:132
  78.0 20.6 %copy-start = (f32[128,1024]{1,0:T(8,128)S(1)}, f32[128,1024]{1,0:T(8,128)}, u32[]{:S(2)}) copy-start(f32[128,1024]{1,0:T(8,128)} %inverse_ref.1) | copy-start | bytes 1572868
  78.1 8.2 %collective-permute-start.14 = (f32[256,128]{1,0:T(8,128)S(1)}, f32[256,128]{1,0:T(8,128)S(1)}, u32[]{:S(2)}, u32[]{:S(2)}) collective-permute-start(f32[256,128]{1,0:T(8,128)S(1)} %get-tuple-element.13), channel_id=1, source_target_pairs={{0,12},{4,0},{8,4},{12,8},{1,13},{5,1},{9,5},{13,9},{2,14},{6,2},{... | collective-permute-start | bytes 393224 | tf_op jit(solution)/shard_map/ppermute | solution.py:172
  80.5 6.5 %collective-permute-start.13 = (f32[256,128]{1,0:T(8,128)S(1)}, f32[256,128]{1,0:T(8,128)S(1)}, u32[]{:S(2)}, u32[]{:S(2)}) collective-permute-start(f32[256,128]{1,0:T(8,128)S(1)} %get-tuple-element.14), channel_id=1, source_target_pairs={{0,8},{4,12},{8,0},{12,4},{1,9},{5,13},{9,1},{13,5},{2,10},{6,14},... | collective-permute-start | bytes 393224 | tf_op jit(solution)/shard_map/ppermute | solution.py:172
  81.5 6.9 %collective-permute-start.12 = (f32[256,128]{1,0:T(8,128)S(1)}, f32[256,128]{1,0:T(8,128)S(1)}, u32[]{:S(2)}, u32[]{:S(2)}) collective-permute-start(f32[256,128]{1,0:T(8,128)S(1)} %get-tuple-element.12), channel_id=1, source_target_pairs={{0,4},{4,8},{8,12},{12,0},{1,5},{5,9},{9,13},{13,1},{2,6},{6,10},{... | collective-permute-start | bytes 393224 | tf_op jit(solution)/shard_map/ppermute | solution.py:172
  82.0 16.5 %collective-permute-start.20 = (f32[128,512]{1,0:T(8,128)S(1)}, f32[128,512]{1,0:T(8,128)S(1)}, u32[]{:S(2)}, u32[]{:S(2)}) collective-permute-start(f32[128,512]{1,0:T(8,128)S(1)} %slice.24), channel_id=1, source_target_pairs={{0,16},{16,32},{32,48},{48,64},{64,80},{80,96},{96,112},{112,0},{1... | collective-permute-start | bytes 786440 | tf_op jit(solution)/shard_map/ppermute | solution.py:136
  82.7 15.9 %collective-permute-start.21 = (f32[128,512]{1,0:T(8,128)S(1)}, f32[128,512]{1,0:T(8,128)S(1)}, u32[]{:S(2)}, u32[]{:S(2)}) collective-permute-start(f32[128,512]{1,0:T(8,128)S(1)} %slice.25), channel_id=1, source_target_pairs={{0,112},{16,0},{32,16},{48,32},{64,48},{80,64},{96,80},{112,96},{1... | collective-permute-start | bytes 786440 | tf_op jit(solution)/shard_map/ppermute | solution.py:137
  88.4 5.4 %collective-permute-start.15 = (f32[320,128]{1,0:T(8,128)S(1)}, f32[320,128]{1,0:T(8,128)S(1)}, u32[]{:S(2)}, u32[]{:S(2)}) collective-permute-start(f32[320,128]{1,0:T(8,128)S(1)} %pad_maximum_fusion), channel_id=1, source_target_pairs={{0,1},{1,2},{2,3},{3,0},{4,5},{5,6},{6,7},{7,4},{8,9},{9,10},{10,1... | collective-permute-start | bytes 491528 | tf_op jit(solution)/shard_map/ppermute | solution.py:181
  89.9 6.9 %collective-permute-start.16 = (f32[320,128]{1,0:T(8,128)S(1)}, f32[320,128]{1,0:T(8,128)S(1)}, u32[]{:S(2)}, u32[]{:S(2)}) collective-permute-start(f32[320,128]{1,0:T(8,128)S(1)} %pad_maximum_fusion), channel_id=1, source_target_pairs={{0,2},{1,3},{2,0},{3,1},{4,6},{5,7},{6,4},{7,5},{8,10},{9,11},{10,... | collective-permute-start | bytes 491528 | tf_op jit(solution)/shard_map/ppermute | solution.py:181
  92.2 6.2 %collective-permute-start.17 = (f32[320,128]{1,0:T(8,128)S(1)}, f32[320,128]{1,0:T(8,128)S(1)}, u32[]{:S(2)}, u32[]{:S(2)}) collective-permute-start(f32[320,128]{1,0:T(8,128)S(1)} %pad_maximum_fusion), channel_id=1, source_target_pairs={{0,3},{1,0},{2,1},{3,2},{4,7},{5,4},{6,5},{7,6},{8,11},{9,8},{10,9... | collective-permute-start | bytes 491528 | tf_op jit(solution)/shard_map/ppermute | solution.py:181
